TPU v7x, 256 devices: a whole 4x4x8 slice. The times are simulated.
256 devices in a mesh: frame: 16 (over x_hi, y, core), row: 16 (over x_lo, z).
Axes of the slice: x: 4 (x_hi: 2, x_lo: 2; x = x_hi * 2 + x_lo), y: 4, z: 8, core: 2. Of those that a mesh axis runs over, the one named last changes fastest.
Arguments:
- proj: bfloat16 [16, 2048, 12288], P('frame', 'row'), may hold values from -6 to 6
- dout: bfloat16 [16, 2048, 4096], P('frame', 'row'), may hold values from -6 to 6
- filt: float32 [4096, 2048], P('row'), may hold values from -0.125 to 0.125
- out_weight: bfloat16 [4096, 4096], P('row', 'frame'), may hold values from -0.09375 to 0.09375
Outputs:
- grad_proj: bfloat16 [16, 2048, 12288], P('frame', 'row')
- grad_out_weight: float32 [4096, 4096], P('row', 'frame')
- grad_filter: float32 [4096, 2048], P('row', 'frame')
All inputs are finite; a program needn't handle non-finite values.
Results may differ from a plain program's by a relative error of at most 0.0049.
Values may be sent and summed in bfloat16 or wider, within the bound.
A program may use at most 128 MiB of HBM per device.

v0:
```python
import math

import jax
import jax.numpy as jnp
from jax import lax
from jax.sharding import PartitionSpec as P

D = 4096
LR = 64
LC = 32


HIGH = lax.Precision.HIGH


def tables(length):
    steps = jnp.arange(length, dtype=jnp.int32)
    product = steps[:, None] * steps[None, :] % length
    angle = product.astype(jnp.float32) * (2.0 * math.pi / length)
    return (jnp.cos(angle), jnp.sin(angle))


def build_tables():
    cos_r, sin_r = tables(LR)
    cos_c, sin_c = tables(LC)
    col_fwd = jnp.stack([cos_c, -sin_c], axis=1)
    row_fwd = jnp.stack(
        [jnp.stack([cos_r, sin_r], axis=1), jnp.stack([-sin_r, cos_r], axis=1)], axis=0
    )
    row_inv = jnp.stack(
        [jnp.stack([cos_r, -sin_r], axis=1), jnp.stack([sin_r, cos_r], axis=1)], axis=0
    )
    col_inv = jnp.stack([cos_c, -sin_c], axis=0) / (LR * LC)
    return (col_fwd, row_fwd, row_inv, col_inv)


def forward_dft(plane, col_fwd, row_fwd):
    part = jnp.einsum("...ijn,jpl->...piln", plane, col_fwd, precision=HIGH)
    return jnp.einsum("qkpi,...piln->...qkln", row_fwd, part, precision=HIGH)


def inverse_dft(spec, row_inv, col_inv):
    back = jnp.einsum("qipk,...pkln->...qiln", row_inv, spec, precision=HIGH)
    return jnp.einsum("...piln,plj->...ijn", back, col_inv, precision=HIGH)


def spec_product(left, right, conjugate):
    left_re = left[..., 0, :, :, :]
    left_im = left[..., 1, :, :, :]
    right_re = right[..., 0, :, :, :]
    right_im = right[..., 1, :, :, :]
    if conjugate:
        real_part = left_re * right_re + left_im * right_im
        imag_part = left_im * right_re - left_re * right_im
    else:
        real_part = left_re * right_re - left_im * right_im
        imag_part = left_re * right_im + left_im * right_re
    return jnp.stack([real_part, imag_part], axis=-4)


def local(proj, dout, filt, out_weight):
    frames_dev = proj.shape[0]
    frame_count = lax.axis_size("frame")
    channels = filt.shape[0]
    col_fwd, row_fwd, row_inv, col_inv = build_tables()
    value = proj[:, :, :D]
    gate_a = proj[:, :, D : 2 * D]
    gate_b = proj[:, :, 2 * D :]
    mixed = (gate_a.astype(jnp.float32) * value.astype(jnp.float32)).astype(jnp.bfloat16)
    mixed_ch, gate_ch = (
        lax.all_to_all(mixed, "row", split_axis=2, concat_axis=1, tiled=True),
        lax.all_to_all(gate_b, "row", split_axis=2, concat_axis=1, tiled=True),
    )
    kernel = jnp.transpose(filt.reshape(channels, LR, LC), (1, 2, 0))
    filt_spec = forward_dft(kernel, col_fwd, row_fwd)
    plane = mixed_ch.astype(jnp.float32).reshape(frames_dev, LR, LC, channels)
    mixed_spec = forward_dft(plane, col_fwd, row_fwd)
    conv = inverse_dft(spec_product(mixed_spec, filt_spec, False), row_inv, col_inv)
    gate_plane = gate_ch.astype(jnp.float32).reshape(frames_dev, LR, LC, channels)
    gated = (gate_plane * conv).astype(jnp.bfloat16).reshape(frames_dev, LR * LC, channels)
    slab = lax.all_gather(out_weight, "frame", axis=1, tiled=True)
    piece = lax.all_gather(dout, "row", axis=1, tiled=True)
    term = jnp.einsum("fkd,cd->fkc", piece, slab, preferred_element_type=jnp.float32)
    weight_acc = jnp.einsum("fkc,fkd->cd", gated, piece, preferred_element_type=jnp.float32)
    weight_part = weight_acc
    scale = 1.0 / (frames_dev * frame_count)
    weight_part = weight_part * scale
    dgated_plane = term.reshape(frames_dev, LR, LC, channels)
    dconv = dgated_plane * gate_plane
    dconv_spec = forward_dft(dconv, col_fwd, row_fwd)
    dmixed = inverse_dft(spec_product(dconv_spec, filt_spec, True), row_inv, col_inv)
    cross = jnp.sum(spec_product(dconv_spec, mixed_spec, True), axis=0)
    filter_part = inverse_dft(cross, row_inv, col_inv)
    filter_part = jnp.transpose(filter_part, (2, 0, 1)).reshape(channels, LR * LC) * scale
    grad_out_weight, grad_filter = (
        lax.psum_scatter(weight_part, "frame", scatter_dimension=1, tiled=True),
        lax.psum_scatter(filter_part, "frame", scatter_dimension=1, tiled=True),
    )
    dgate_b = (dgated_plane * conv).astype(jnp.bfloat16).reshape(frames_dev, LR * LC, channels)
    dmixed_b = dmixed.astype(jnp.bfloat16).reshape(frames_dev, LR * LC, channels)
    dmixed_tok, dgate_tok = (
        lax.all_to_all(dmixed_b, "row", split_axis=1, concat_axis=2, tiled=True),
        lax.all_to_all(dgate_b, "row", split_axis=1, concat_axis=2, tiled=True),
    )
    dmixed_f = dmixed_tok.astype(jnp.float32)
    grad_value = (dmixed_f * gate_a.astype(jnp.float32)).astype(jnp.bfloat16)
    grad_gate = (dmixed_f * value.astype(jnp.float32)).astype(jnp.bfloat16)
    grad_proj = jnp.concatenate([grad_value, grad_gate, dgate_tok], axis=2)
    return (grad_proj, grad_out_weight, grad_filter)


def solution(mesh):
    placed = (P("frame", "row", None), P("frame", "row", None), P("row", None), P("row", "frame"))
    return jax.shard_map(
        local,
        mesh=mesh,
        in_specs=placed,
        out_specs=(P("frame", "row", None), P("row", "frame"), P("row", "frame")),
        check_vma=False,
    )
```

profile of v0, /device:TPU:32, one launch (start us, length us, event | category | flops | bytes accessed | tf_op | source)
XLA Modules:
  0.0 488.1 jit_solution(10425061957932197084)
XLA Ops:
  8.6 3.5 fusion.117
  12.2 2.8 copy.99
  15.5 22.4 %reduce = bf16[4096,128]{1,0:T(8,128)(2,1)S(1)} reduce(bf16[4096,1,128]{2,1,0:T(2,128)(2,1)S(1)} %bitcast.253, bf16[]{:T(256)} %broadcast.286), dimensions={1}, to_apply=%bitcast.224.reduce_sub_computation | reduce | bytes 2097154
  39.1 10.1 %all-to-all-start = ((bf16[16,2,16384]{2,1,0:T(2,128)(2,1)}), bf16[16,2,16384]{2,1,0:T(2,128)(2,1)}, u32[]{:S(2)}, u32[]{:S(2)}) async-start(bf16[16,2,16384]{2,1,0:T(2,128)(2,1)} %reshape.398), calls=%async_computation | async-start | bytes 2097152 | tf_op jit(solution)/shard_map/all_to_all | solution.py:72
  50.8 17.0 %copy.138 = bf16[1,128,4096]{1,0,2:T(2,128)(2,1)} copy(bf16[1,128,4096]{1,2,0:T(8,128)(2,1)S(1)} %fusion.45) | data formatting | bytes 2097152 | tf_op jit(solution)/shard_map/convert_element_type | solution.py:69
  67.9 23.4 %reduce.1 = bf16[4096,128]{1,0:T(8,128)(2,1)S(1)} reduce(bf16[4096,1,128]{2,1,0:T(2,128)(2,1)} %bitcast.255, bf16[]{:T(256)} %broadcast.286), dimensions={1}, to_apply=%bitcast.243.reduce_sub_computation | reduce | bytes 2097154
  92.5 8.3 %all-to-all-start.2 = ((bf16[16,2,16384]{2,1,0:T(2,128)(2,1)}), bf16[16,2,16384]{2,1,0:T(2,128)(2,1)}, u32[]{:S(2)}, u32[]{:S(2)}) async-start(bf16[16,2,16384]{2,1,0:T(2,128)(2,1)} %reshape.394), calls=%async_computation.2 | async-start | bytes 2097152 | tf_op jit(solution)/shard_map/all_to_all | solution.py:71
  101.3 1.9 copy.53
  103.7 4.3 reshape.399
  108.0 3.2 bitcast_convert_fusion.1
  111.3 1.9 copy.51
  113.2 23.0 %all-to-all-done.2 = bf16[16,2,16384]{2,1,0:T(2,128)(2,1)} async-done(((bf16[16,2,16384]{2,1,0:T(2,128)(2,1)}), bf16[16,2,16384]{2,1,0:T(2,128)(2,1)}, u32[]{:S(2)}, u32[]{:S(2)}) %all-to-all-start.2) | async-done | bytes 1048608 | tf_op jit(solution)/shard_map/all_to_all | solution.py:71
  136.2 5.8 %reshape.395 = bf16[4096,1,128]{2,1,0:T(2,128)(2,1)} reshape(bf16[16,2,16384]{2,1,0:T(2,128)(2,1)} %all-to-all-done.2) | data formatting | bytes 2097152
  142.0 2.7 copy.95
  144.7 2.3 copy.62
  147.0 2.5 convolution_bitcast_fusion
  149.4 5.3 %fusion.36 = f32[1,2,64,32,256]{4,2,1,3,0:T(8,128)} fusion(f32[2,64,32,256,1]{3,2,1,0,4:T(8,128)S(1)} %convolution_bitcast_fusion, f32[1,64,2,64]{3,1,2,0:T(8,128)S(1)} %get-tuple-element.25, f32[1,64,2,64]{3,1,2,0:T(8,128)S(1)} %get-tuple-element.28), kind=kOutput, calls=%fused_computation.35 | convolution fusion | flops 805322752 | bytes 8454144 | tf_op jit(solution)/shard_map/qkpi,...piln->...qkln/dot_general | solution.py:39
  154.7 121.0 %all-gather.3.cloned.1.call-done = bf16[1,2048,4096]{2,1,0:T(8,128)(2,1)} async-done(((bf16[1,128,4096]{2,1,0:T(8,128)(2,1)}), bf16[1,2048,4096]{2,1,0:T(8,128)(2,1)}) %all-gather.3.cloned.1.call-update) | async-done | bytes 16777232 | tf_op jit(solution)/shard_map/all_gather | solution.py:82
  275.8 8.9 %fusion.2 = f32[2048,256]{1,0:T(8,128)S(1)} fusion(bf16[256,4096]{1,0:T(8,128)(2,1)} %all-gather.5.cloned.1.call-done, bf16[1,2048,4096]{2,1,0:T(8,128)(2,1)} %all-gather.3.cloned.1.call-done), kind=kOutput, calls=%fused_computation.2 | convolution fusion | flops 4294967296 | bytes 20971520 | tf_op jit(solution)/shard_map/fkd,cd->fkc/dot_general | solution.py:83
  286.0 1.8 convolution_bitcast_fusion.2
  287.8 4.3 fusion.27
  294.5 2.2 fusion.42
  296.7 5.3 %bitcast_multiply_fusion = f32[32,64,256]{2,0,1:T(8,128)} fusion(f32[2,64,32,256]{3,1,2,0:T(8,128)S(1)} %fusion.42, f32[1,32,32]{1,2,0:T(8,128)S(1)} %get-tuple-element.34, f32[1,32,32]{1,2,0:T(8,128)S(1)} %get-tuple-element.35), kind=kOutput, calls=%fused_computation.44 | convolution fusion | flops 201854976 | bytes 6299648 | tf_op jit(solution)/shard_map/...piln,plj->...ijn/dot_general | solution.py:44
  301.9 2.9 copy.69
  304.9 3.4 convolution_bitcast_fusion.1
  308.3 6.1 %fusion.30 = f32[2,64,32,256]{3,1,2,0:T(8,128)} fusion(f32[2,64,32,256]{3,2,1,0:T(8,128)S(1)} %convolution_bitcast_fusion.1, f32[1,64,2,64]{3,1,2,0:T(8,128)S(1)} %get-tuple-element.25, f32[1,64,2,64]{3,1,2,0:T(8,128)S(1)} %get-tuple-element.28), kind=kOutput, calls=%fused_computation.33 | convolution fusion | flops 805322752 | bytes 8454144 | tf_op jit(solution)/shard_map/qkpi,...piln->...qkln/dot_general | solution.py:39
  314.4 6.5 %fusion.53 = (f32[1,1,64,32,256]{4,2,3,1,0:T(8,128)}, f32[1,1,64,32,256]{4,2,3,1,0:T(8,128)}, f32[1,1,64,32,256]{4,2,3,1,0:T(8,128)S(1)}, f32[1,1,64,32,256]{4,2,3,1,0:T(8,128)}) fusion(f32[2,64,32,256]{3,1,2,0:T(8,128)} %fusion.30, f32[1,2,64,32,256]{4,2,1,3,0:T(8,128)S(1)} %copy-done.3, f32[1,2,64,32,256]{4,2,1,3,0:T(8,128)S(1)} %copy-done.1), kind=kLoop, calls=%fused_computation.61 | loop fusion | flops 6291456 | bytes 20971520 | tf_op jit(solution)/shard_map/stack | solution.py:58
  321.0 3.7 fusion.39
  324.7 4.8 fusion.47
  329.5 11.6 %copy.137 = bf16[1,2048,256]{2,0,1:T(2,128)(2,1)S(1)} copy(bf16[1,2048,256]{2,1,0:T(8,128)(2,1)S(1)} %bitcast.260) | data formatting | bytes 2097152 | tf_op jit(solution)/shard_map/reshape | solution.py:99
  341.1 11.6 %reduce.2 = bf16[2048,256]{1,0:T(8,128)(2,1)} reduce(bf16[2048,1,256]{2,1,0:T(2,128)(2,1)S(1)} %bitcast.257, bf16[]{:T(256)} %broadcast.286), dimensions={1}, to_apply=%bitcast.242.reduce_sub_computation | reduce | bytes 2097154
  352.8 2.2 reshape.396
  355.0 7.4 %all-to-all-start.3 = ((bf16[16,2,16384]{2,1,0:T(2,128)(2,1)}), bf16[16,2,16384]{2,1,0:T(2,128)(2,1)}, u32[]{:S(2)}, u32[]{:S(2)}) async-start(bf16[16,2,16384]{2,1,0:T(2,128)(2,1)} %reshape.396), calls=%async_computation.3 | async-start | bytes 2097152 | tf_op jit(solution)/shard_map/all_to_all | solution.py:103
  362.5 10.5 %fusion.4 = f32[256,4096]{1,0:T(8,128)} fusion(bf16[2048,256]{1,0:T(8,128)(2,1)S(1)} %bitcast.259, bf16[1,2048,4096]{2,1,0:T(8,128)(2,1)} %all-gather.3.cloned.1.call-done), kind=kOutput, calls=%fused_computation.4 | convolution fusion | flops 4296015872 | bytes 22020096 | tf_op jit(solution)/shard_map/fkc,fkd->cd/dot_general | solution.py:84
  374.6 3.6 fusion.33
  378.2 3.5 bitcast_convert_fusion
  381.7 11.7 %copy.139 = bf16[1,2048,256]{2,0,1:T(2,128)(2,1)S(1)} copy(bf16[1,2048,256]{2,1,0:T(8,128)(2,1)S(1)} %bitcast.261) | data formatting | bytes 2097152 | tf_op jit(solution)/shard_map/reshape | solution.py:100
  393.4 11.6 %reduce.3 = bf16[2048,256]{1,0:T(8,128)(2,1)} reduce(bf16[2048,1,256]{2,1,0:T(2,128)(2,1)S(1)} %bitcast.254, bf16[]{:T(256)} %broadcast.286), dimensions={1}, to_apply=%bitcast.244.reduce_sub_computation | reduce | bytes 2097154
  405.0 2.2 reshape.400
  407.2 8.5 %all-to-all-start.1 = ((bf16[16,2,16384]{2,1,0:T(2,128)(2,1)}), bf16[16,2,16384]{2,1,0:T(2,128)(2,1)}, u32[]{:S(2)}, u32[]{:S(2)}) async-start(bf16[16,2,16384]{2,1,0:T(2,128)(2,1)} %reshape.400), calls=%async_computation.1 | async-start | bytes 2097152 | tf_op jit(solution)/shard_map/all_to_all | solution.py:102
  415.7 4.3 reshape.397
  422.8 18.9 %all-to-all-done.1 = bf16[16,2,16384]{2,1,0:T(2,128)(2,1)} async-done(((bf16[16,2,16384]{2,1,0:T(2,128)(2,1)}), bf16[16,2,16384]{2,1,0:T(2,128)(2,1)}, u32[]{:S(2)}, u32[]{:S(2)}) %all-to-all-start.1) | async-done | bytes 1048608 | tf_op jit(solution)/shard_map/all_to_all | solution.py:102
  441.6 5.8 %reshape.401 = bf16[2048,1,256]{2,1,0:T(2,128)(2,1)} reshape(bf16[16,2,16384]{2,1,0:T(2,128)(2,1)} %all-to-all-done.1) | data formatting | bytes 2097152
  447.4 6.2 %copy.58 = f32[1,16,128,256]{2,3,1,0:T(8,128)} copy(bf16[1,16,128,256]{3,0,2,1:T(2,128)(2,1)} %bitcast.258) | data formatting | bytes 3145728 | tf_op jit(solution)/shard_map/convert_element_type | solution.py:105
  453.6 2.0 fusion.43
  455.7 16.4 %pad_maximum_fusion = bf16[1,128,12288]{1,2,0:T(8,128)(2,1)} fusion(bf16[1,128,4096]{1,2,0:T(8,128)(2,1)S(1)} %bitcast.265, bf16[1,128,4096]{1,2,0:T(8,128)(2,1)S(1)} %get-tuple-element.23, bf16[1,128,4096]{1,2,0:T(8,128)(2,1)S(1)} %get-tuple-element.22), kind=kLoop, calls=%fused_computation.28 | loop fusion | flops 9437184 | bytes 6291456 | tf_op jit(solution)/shard_map/concatenate | solution.py:108
  472.1 4.6 copy.70
  476.7 4.6 reduce-scatter.3.cloned.1.call-done
  (52 shorter events, 15.0 us)
Async XLA Ops:
  7.2 147.6 %all-gather.5.cloned.1.call-start = ((), (), s32[]{:S(2)}) async-start(), calls=%async_computation.7 | async-start | bytes 2228224 | tf_op jit(solution)/shard_map/all_gather | solution.py:81
  7.9 267.9 %all-gather.3.cloned.1.call-start = ((), (), s32[]{:S(2)}) async-start(), calls=%async_computation.6 | async-start | bytes 17825792 | tf_op jit(solution)/shard_map/all_gather | solution.py:82
  37.9 11.2 %copy-start.11 = (bf16[1,128,4096]{2,1,0:T(8,128)(2,1)S(1)}, bf16[1,128,4096]{2,1,0:T(8,128)(2,1)}, u32[]{:S(2)}) copy-start(bf16[1,128,4096]{2,1,0:T(8,128)(2,1)} %get-tuple-element.19) | copy-start | bytes 3145732
  39.1 10.8 %copy-start.10 = (bf16[1,128,4096]{2,1,0:T(8,128)(2,1)S(1)}, bf16[1,128,4096]{2,1,0:T(8,128)(2,1)}, u32[]{:S(2)}) copy-start(bf16[1,128,4096]{2,1,0:T(8,128)(2,1)} %get-tuple-element.18) | copy-start | bytes 3145732
  39.1 53.4 %all-to-all-start = ((bf16[16,2,16384]{2,1,0:T(2,128)(2,1)}), bf16[16,2,16384]{2,1,0:T(2,128)(2,1)}, u32[]{:S(2)}, u32[]{:S(2)}) async-start(bf16[16,2,16384]{2,1,0:T(2,128)(2,1)} %reshape.398), calls=%async_computation | async-start | bytes 2097152 | tf_op jit(solution)/shard_map/all_to_all | solution.py:72
  50.5 17.3 %copy-start.4 = (bf16[1,128,4096]{1,2,0:T(8,128)(2,1)}, bf16[1,128,4096]{1,2,0:T(8,128)(2,1)S(1)}, u32[]{:S(2)}) copy-start(bf16[1,128,4096]{1,2,0:T(8,128)(2,1)S(1)} %copy.97) | copy-start | bytes 3145732
  92.5 8.8 %copy-start.12 = (f32[256,2048]{1,0:T(8,128)S(1)}, f32[256,2048]{1,0:T(8,128)}, u32[]{:S(2)}) copy-start(f32[256,2048]{1,0:T(8,128)} %param.6) | copy-start | bytes 6291460
  92.5 43.7 %all-to-all-start.2 = ((bf16[16,2,16384]{2,1,0:T(2,128)(2,1)}), bf16[16,2,16384]{2,1,0:T(2,128)(2,1)}, u32[]{:S(2)}, u32[]{:S(2)}) async-start(bf16[16,2,16384]{2,1,0:T(2,128)(2,1)} %reshape.394), calls=%async_computation.2 | async-start | bytes 2097152 | tf_op jit(solution)/shard_map/all_to_all | solution.py:71
  100.7 376.0 %reduce-scatter.5.cloned.1.call-start = ((), (), s32[]{:S(2)}) async-start(), calls=%async_computation.9 | async-start | bytes 2228224 | tf_op jit(solution)/shard_map/reduce_scatter | solution.py:97
  284.7 1.3 copy-start.6
  287.8 4.3 copy-start
  292.1 2.3 copy-start.2
  308.3 6.2 %copy-start.1 = (f32[1,2,64,32,256]{4,2,1,3,0:T(8,128)S(1)}, f32[1,2,64,32,256]{4,2,1,3,0:T(8,128)}, u32[]{:S(2)}) copy-start(f32[1,2,64,32,256]{4,2,1,3,0:T(8,128)} %fusion.36) | copy-start | bytes 12582916
  308.3 6.1 %copy-start.3 = (f32[1,2,64,32,256]{4,2,1,3,0:T(8,128)S(1)}, f32[1,2,64,32,256]{4,2,1,3,0:T(8,128)}, u32[]{:S(2)}) copy-start(f32[1,2,64,32,256]{4,2,1,3,0:T(8,128)} %copy-done.2) | copy-start | bytes 12582916
  321.0 3.7 copy-start.7
  352.8 9.7 %copy-start.9 = (bf16[1,64,32,256]{3,2,1,0:T(8,128)(2,1)S(1)}, bf16[1,64,32,256]{3,2,1,0:T(8,128)(2,1)}, u32[]{:S(2)}) copy-start(bf16[1,64,32,256]{3,2,1,0:T(8,128)(2,1)} %get-tuple-element.20) | copy-start | bytes 3145732
  355.0 52.1 %all-to-all-start.3 = ((bf16[16,2,16384]{2,1,0:T(2,128)(2,1)}), bf16[16,2,16384]{2,1,0:T(2,128)(2,1)}, u32[]{:S(2)}, u32[]{:S(2)}) async-start(bf16[16,2,16384]{2,1,0:T(2,128)(2,1)} %reshape.396), calls=%async_computation.3 | async-start | bytes 2097152 | tf_op jit(solution)/shard_map/all_to_all | solution.py:103
  362.5 118.8 %reduce-scatter.3.cloned.1.call-start = ((), (), s32[]{:S(2)}) async-start(), calls=%async_computation.8 | async-start | bytes 4456448 | tf_op jit(solution)/shard_map/reduce_scatter | solution.py:96
  373.0 1.6 copy-start.8
  407.2 34.5 %all-to-all-start.1 = ((bf16[16,2,16384]{2,1,0:T(2,128)(2,1)}), bf16[16,2,16384]{2,1,0:T(2,128)(2,1)}, u32[]{:S(2)}, u32[]{:S(2)}) async-start(bf16[16,2,16384]{2,1,0:T(2,128)(2,1)} %reshape.400), calls=%async_computation.1 | async-start | bytes 2097152 | tf_op jit(solution)/shard_map/all_to_all | solution.py:102
  447.4 6.2 %copy-start.5 = (bf16[1,128,4096]{1,2,0:T(8,128)(2,1)S(1)}, bf16[1,128,4096]{1,2,0:T(8,128)(2,1)}, u32[]{:S(2)}) copy-start(bf16[1,128,4096]{1,2,0:T(8,128)(2,1)} %copy-done.4) | copy-start | bytes 3145732
Sparse Core Ops, SparseCore 0:
  10.6 59.2 all-gather.4
  71.7 204.0 all-gather.2
  305.0 79.4 reduce-scatter.4
  389.9 91.4 reduce-scatter.2
where the time goes:
time: 494 us; the launch traced here: 488 us
  waiting for transfers between devices  169 us (34%)
  local copies, waits for them, and re-layouts  105 us (21%)
  other arithmetic  99.3 us (20%)
  matrix products  65.8 us (13%)
  starting transfers between devices  35 us (7%)
  between operations  14.3 us (3%)
    all_gather x1, waiting for transfers between devices, local(): piece = lax.all_gather(dout, 'row', axis=1, tiled=True)  121 us
    unnamed x4, other arithmetic  69 us
    unnamed x42, local copies, waits for them, and re-layouts  45.9 us
    all_to_all x1, waiting for transfers between devices, local(): lax.all_to_all(mixed, 'row', split_axis=2, concat_axis=1, tiled=True)  23 us
    all_to_all x1, waiting for transfers between devices, local(): lax.all_to_all(dmixed_b, 'row', split_axis=1, concat_axis=2, tiled=True)  18.9 us
    convert_element_type x1, local copies, waits for them, and re-layouts, local(): (gate_a.astype(jnp.float32) * value.astype(jnp.float32)).astype(jnp.bfloa...  17 us
    concatenate x1, other arithmetic, local(): grad_proj = jnp.concatenate([grad_value, grad_gate, dgate_tok], axis=2)  16.4 us
    dot_general x3, matrix products, forward_dft(): return jnp.einsum('qkpi,...piln->...qkln', row_fwd, part, precision=HIGH)  15.7 us
  transfers between devices with their start and end apart: 8, of which 4 were waited for; matrix products, arithmetic and copies ran while one was open for 49% of the time, Pallas kernels for 0%

commit v1 on v0

v1 whole, which is shorter than its diff:
```python
import functools

import jax
import jax.numpy as jnp
import ml_dtypes
import numpy as np
from jax import lax
from jax.experimental import pallas as pl
from jax.experimental.pallas import tpu as pltpu
from jax.sharding import PartitionSpec as P

LR = 64
LC = 32
POS = LR * LC
HALF = POS // 2
G = 8
MESH = pl.DeviceIdType.MESH
BF = jnp.bfloat16
F32 = jnp.float32


def split_table(table):
    high = table.astype(ml_dtypes.bfloat16)
    low = (table - high.astype(np.float64)).astype(ml_dtypes.bfloat16)
    return high, low


def build_tables():
    j = np.arange(LC)
    fwd = np.zeros((LC, LC))
    inv = np.zeros((LC, LC))
    fwd[0], inv[:, 0] = 1.0, 1.0
    fwd[1] = np.cos(np.pi * j)
    inv[:, 1] = np.cos(np.pi * j)
    for l in range(1, LC // 2):
        angle = 2 * np.pi * ((j * l) % LC) / LC
        fwd[2 * l], fwd[2 * l + 1] = np.cos(angle), -np.sin(angle)
        inv[:, 2 * l], inv[:, 2 * l + 1] = 2 * np.cos(angle), -2 * np.sin(angle)
    inv = inv / POS
    eye = np.eye(G)
    col_fwd = np.einsum("qj,ab->qabj", fwd, eye).reshape(G * LC, G * LC)
    col_inv = np.einsum("jq,ab->ajqb", inv, eye).reshape(G * LC, G * LC)
    i = np.arange(LR)
    angle = 2 * np.pi * ((i[:, None] * i[None, :]) % LR) / LR
    c, s = np.cos(angle), np.sin(angle)
    o = np.zeros_like(c)
    row_fwd = np.block([[c, s], [-s, c]])
    row_inv = np.block([[c, -s], [s, c]])
    edge_fwd = np.block([[c, o], [-s, o], [o, c], [o, -s]])
    edge_inv = np.block([[c, -s, o, o], [o, o, c, -s]])
    out = []
    for table in (col_fwd, row_fwd, edge_fwd, row_inv, edge_inv, col_inv):
        out.extend(split_table(table))
    return tuple(out)


def split(x):
    high = x.astype(BF)
    return high, (x - high.astype(F32)).astype(BF)


def dot(a, b):
    return jnp.dot(a, b, preferred_element_type=F32)


def dot_t(a, b):
    return lax.dot_general(a, b, (((1,), (1,)), ((), ())), preferred_element_type=F32)


def dot3(high, low, x, product=dot):
    x_high, x_low = split(x)
    return product(high, x_high) + product(high, x_low) + product(low, x_high)


def kernel(
    R, F, D,
    proj, dout, w, filt,
    a1h, a1l, a2h, a2l, azh, azl, b2h, b2l, bzh, bzl, b1h, b1l,
    out, gw_out, gf_out,
    value, gate_a, mx, mch, gmn, cmn, cvo, dh, w2, fsp, msp, dsp, tmp, gt, dcv, dch, dg, dms, dmt, gws, gwr, gfs, gfr,
    local, ring_s, ring_r, mx_s, mx_r, gate_s, gate_r, w_s, w_r, x_s, x_r, dg_s, dg_r, dm_s, dm_r, gw_s, gw_r, gf_s, gf_r,
):
    NZ = R // 2
    TB, CB, DB, PB = POS // R, D // R, D // F, POS // F
    f, r = lax.axis_index("frame"), lax.axis_index("row")
    xl, z = lax.div(r, NZ), lax.rem(r, NZ)
    pr = (1 - xl) * NZ + z
    right = xl * NZ + lax.rem(z + 1, NZ)
    left = xl * NZ + lax.rem(z + NZ - 1, NZ)

    def at(index, size):
        return pl.ds(pl.multiple_of(index * size, size), size)

    def remote(src, dst, send, recv, frame, row):
        return pltpu.make_async_remote_copy(
            src_ref=src, dst_ref=dst, send_sem=send, recv_sem=recv,
            device_id={"frame": frame, "row": row}, device_id_type=MESH,
        )

    def loop(start, stop, step):
        def body(k, carry):
            step(k)
            return carry

        lax.fori_loop(start, stop, body, 0)

    own_dout = pltpu.make_async_copy(dout, dh.at[at(z, TB), :], local.at[0])
    own_w = pltpu.make_async_copy(w, w2.at[pl.ds(0, CB), at(f, DB)], local.at[1])
    own_gate = [
        pltpu.make_async_copy(proj.at[:, at(2 * R + c, CB)], gmn.at[n, at(z, TB), :], local.at[2 + n])
        for n, c in enumerate((r, pr))
    ]
    own_value = pltpu.make_async_copy(proj.at[:, pl.ds(0, D)], value, local.at[8])
    own_a = pltpu.make_async_copy(proj.at[:, pl.ds(D, D)], gate_a, local.at[9])
    own_value.start()
    own_a.start()
    own_dout.start()
    own_w.start()
    for copy in own_gate:
        copy.start()

    barrier = pltpu.get_barrier_semaphore()

    def greet(frame, row):
        pl.semaphore_signal(barrier, inc=1, device_id={"frame": frame, "row": row}, device_id_type=MESH)

    loop(1, R, lambda k: greet(f, lax.rem(r + k, R)))

    def greet_plane(k):
        greet(lax.rem(f + k, F), r)
        greet(lax.rem(f + k, F), pr)

    loop(1, F, greet_plane)

    own_value.wait()
    own_a.wait()
    mx[...] = (value[...].astype(F32) * gate_a[...].astype(F32)).astype(BF)
    own_mx = pltpu.make_async_copy(mx.at[:, at(r, CB)], mch.at[at(r, TB), :], local.at[4])
    own_mx.start()
    own_dout.wait()
    pl.semaphore_wait(barrier, (R - 1) + 2 * (F - 1))

    def ring_copy(way, step, block):
        rows = pl.ds(pl.multiple_of(block * TB + way * (TB // 2), TB // 2), TB // 2)
        place = dh.at[rows, :]
        return remote(place, place, ring_s.at[way, step], ring_r.at[way, step], f, (right, left)[way])

    def ring_block(way, step):
        return lax.rem(z + NZ - step, NZ) if way == 0 else lax.rem(z + step, NZ)

    def ring(step):
        if step < NZ:
            for way in range(2):
                if step > 0:
                    ring_copy(way, step - 1, ring_block(way, step)).wait_recv()
                if step < NZ - 1:
                    ring_copy(way, step, ring_block(way, step)).start()

    def mx_copy(peer, sender):
        return remote(mx.at[:, at(peer, CB)], mch.at[at(sender, TB), :], mx_s.at[peer], mx_r.at[sender], f, peer)

    def gate_copy(n, peer_z, sender_z):
        c = (xl if n == 0 else 1 - xl) * NZ + peer_z
        return remote(
            proj.at[:, at(2 * R + c, CB)], gmn.at[n, at(sender_z, TB), :],
            gate_s.at[n, peer_z], gate_r.at[n, sender_z], f, xl * NZ + peer_z,
        )

    def w_copy(n, peer, sender):
        return remote(
            w, w2.at[pl.ds(n * CB, CB), at(sender, DB)], w_s.at[n, peer], w_r.at[n, sender], peer, (r, pr)[n]
        )

    def send_w(k):
        peer = lax.rem(f + k, F)
        w_copy(0, peer, f).start()
        w_copy(1, peer, f).start()

    ring(0)

    def send_mx(k):
        peer = lax.rem(r + k, R)
        mx_copy(peer, r).start()

    loop(1, R, send_mx)

    def send_gate(k):
        peer = lax.rem(z + k, NZ)
        gate_copy(0, peer, z).start()
        gate_copy(1, peer, z).start()

    loop(1, NZ, send_gate)
    w_copy(1, f, f).start()
    loop(1, F, send_w)

    def columns(k, part):
        tmp[:, at(k, G), :] = part.reshape(LC, G, CB)

    def pair(ref, index):
        return ref[pl.ds(index, 2)].reshape(2 * LR, CB)

    def rows_fwd(dst):
        edge = dot3(azh[...], azl[...], pair(tmp, 0)).reshape(4, LR, CB)
        dst[0:2] = edge[0:2]
        dst[LC : LC + 2] = edge[2:4]

        def step(l):
            dst[pl.ds(2 * l, 2)] = dot3(a2h[...], a2l[...], pair(tmp, 2 * l)).reshape(2, LR, CB)

        loop(1, LC // 2, step)

    def multiply(a, b, index, conjugate):
        are, aim, bre, bim = a[index], a[index + 1], b[index], b[index + 1]
        if conjugate:
            return are * bre + aim * bim, aim * bre - are * bim
        return are * bre - aim * bim, are * bim + aim * bre

    def rows_inv(a, b, conjugate):
        first, last = multiply(a, b, 0, conjugate), multiply(a, b, LC, conjugate)
        edge = jnp.concatenate(first + last, axis=0)
        tmp[0:2] = dot3(bzh[...], bzl[...], edge).reshape(2, LR, CB)

        def step(l):
            both = jnp.concatenate(multiply(a, b, 2 * l, conjugate), axis=0)
            tmp[pl.ds(2 * l, 2)] = dot3(b2h[...], b2l[...], both).reshape(2, LR, CB)

        loop(1, LC // 2, step)

    def columns_inv(k):
        return dot3(b1h[...], b1l[...], tmp[:, at(k, G), :].reshape(G * LC, CB))

    CH = G * LC
    CHUNKS = POS // CH

    def filt_step(k):
        columns(k, dot3(a1h[...], a1l[...], filt[:, at(k, CH)], dot_t))

    loop(0, CHUNKS, filt_step)
    rows_fwd(fsp)
    ring(1)

    own_mx.wait()

    def wait_mx(k):
        sender = lax.rem(r + R - k, R)
        mx_copy(r, sender).wait_recv()

    loop(1, R, wait_mx)
    ring(2)

    def plane_step(src):
        def step(k):
            x = src[at(k, CH), :]
            columns(k, dot(a1h[...], x) + dot(a1l[...], x))

        return step

    loop(0, CHUNKS, plane_step(mch))
    rows_fwd(msp)
    ring(3)
    rows_inv(msp, fsp, False)

    def conv_step(k):
        cmn[0, at(k, CH), :] = columns_inv(xl * (CHUNKS // 2) + k).astype(BF)
        cvo[at(k, CH), :] = columns_inv((1 - xl) * (CHUNKS // 2) + k).astype(BF)

    loop(0, CHUNKS // 2, conv_step)
    conv_copy = remote(cvo, cmn.at[1], x_s.at[0], x_r.at[0], f, pr)
    conv_copy.start()
    for copy in own_gate:
        copy.wait()
    own_w.wait()
    for step in range(4, NZ):
        ring(step)

    def wait_gate(k):
        sender = lax.rem(z + NZ - k, NZ)
        gate_copy(0, z, sender).wait_recv()
        gate_copy(1, z, sender).wait_recv()

    loop(1, NZ, wait_gate)

    def wait_w(k):
        sender = lax.rem(f + F - k, F)
        w_copy(0, f, sender).wait_recv()
        w_copy(1, f, sender).wait_recv()

    w_copy(1, f, f).wait_recv()
    loop(1, F, wait_w)
    conv_copy.wait_recv()

    def dgated_step(m):
        rows = at(m, CH)
        term = dot_t(dh[rows, :], w2[...])
        for n in range(2):
            d = term[:, n * CB : (n + 1) * CB]
            gate = gmn[n, rows, :].astype(F32)
            conv = cmn[n, rows, :].astype(F32)
            gt[m, pl.ds(n * CB, CB), :] = (gate * conv).T.astype(BF)
            dg[n, rows, :] = (d * conv).astype(BF)
            dconv = (d * gate).astype(BF)
            if n == 0:
                dch[pl.ds(pl.multiple_of(xl * HALF + m * CH, CH), CH), :] = dconv
            else:
                dcv[rows, :] = dconv

    loop(0, HALF // CH, dgated_step)
    dconv_copy = remote(dcv, dch.at[at(xl, HALF), :], x_s.at[1], x_r.at[1], f, pr)
    dconv_copy.start()

    def gw_copy(n, peer, slot):
        return remote(gws.at[peer, n], gwr.at[slot], gw_s.at[n, peer], gw_r.at[slot], peer, (r, pr)[n])

    def gw_step(k):
        peer = lax.rem(f + k, F)
        total = jnp.zeros((2 * CB, DB), F32)
        for m in range(HALF // CH):
            total = total + dot(gt[m], dh[pl.ds(m * CH, CH), at(peer, DB)])
        piece = total.astype(BF)
        gws[peer, 0] = piece[:CB]
        gws[peer, 1] = piece[CB:]
        gw_copy(1, peer, F + f).start()

    def gw_send_step(k):
        gw_step(k)
        gw_copy(0, lax.rem(f + k, F), f).start()

    loop(1, F, gw_send_step)
    gw_step(0)

    def dg_copy(n, peer_z, channel):
        return remote(
            dg.at[n, at(peer_z, TB), :], out.at[:, at(2 * R + channel, CB)],
            dg_s.at[n, peer_z], dg_r.at[channel], f, xl * NZ + peer_z,
        )

    own_dg = [
        pltpu.make_async_copy(dg.at[n, at(z, TB), :], out.at[:, at(2 * R + c, CB)], local.at[5 + n])
        for n, c in enumerate((r, pr))
    ]
    for copy in own_dg:
        copy.start()

    def send_dg(k):
        peer = lax.rem(z + k, NZ)
        dg_copy(0, peer, r).start()
        dg_copy(1, peer, pr).start()

    loop(1, NZ, send_dg)

    dconv_copy.wait_recv()
    loop(0, CHUNKS, plane_step(dch))
    rows_fwd(dsp)
    rows_inv(dsp, fsp, True)

    def dmixed_step(k):
        dms[at(k, CH), :] = columns_inv(k).astype(BF)

    loop(0, CHUNKS, dmixed_step)

    def dm_copy(peer, sender):
        return remote(dms.at[at(peer, TB), :], dmt.at[:, at(sender, CB)], dm_s.at[peer], dm_r.at[sender], f, peer)

    loop(1, R, lambda k: dm_copy(lax.rem(r + k, R), r).start())
    own_dm = pltpu.make_async_copy(dms.at[at(r, TB), :], dmt.at[:, at(r, CB)], local.at[7])
    own_dm.start()

    rows_inv(dsp, msp, True)

    def gf_step(k):
        gfs[at(k, CH), :] = columns_inv(k).astype(BF)

    loop(0, CHUNKS, gf_step)

    def gf_copy(peer, sender):
        return remote(gfs.at[at(peer, PB), :], gfr.at[sender], gf_s.at[peer], gf_r.at[sender], peer, r)

    loop(1, F, lambda k: gf_copy(lax.rem(f + k, F), f).start())

    def finish(c):
        cols = at(c, CB)
        d = dmt[:, cols].astype(F32)
        out[:, cols] = (d * gate_a[:, cols].astype(F32)).astype(BF)
        out[:, at(R + c, CB)] = (d * value[:, cols].astype(F32)).astype(BF)

    own_dm.wait()
    finish(r)

    def dm_step(k):
        sender = lax.rem(r + R - k, R)
        dm_copy(r, sender).wait_recv()
        finish(sender)

    loop(1, R, dm_step)

    gw_out[...] = gws[f, 0].astype(F32)

    def gw_other(sender):
        gw_copy(1, f, F + sender).wait_recv()
        gw_out[...] += gwr[F + sender].astype(F32)

    def gw_arrive(k):
        sender = lax.rem(f + F - k, F)
        gw_copy(0, f, sender).wait_recv()
        gw_out[...] += gwr[sender].astype(F32)
        gw_other(sender)

    loop(1, F, gw_arrive)
    gw_other(f)
    gw_out[...] = gw_out[...] * (1.0 / F)

    gfr[f] = gfs[at(f, PB), :]

    def gf_arrive(k):
        gf_copy(f, lax.rem(f + F - k, F)).wait_recv()

    loop(1, F, gf_arrive)
    total = gfr[0].astype(F32)
    for n in range(1, F):
        total = total + gfr[n].astype(F32)
    gf_out[...] = total.T * (1.0 / F)

    for copy in own_dg:
        copy.wait()

    def dg_arrive(k):
        sender = lax.rem(z + NZ - k, NZ)
        dg_copy(0, z, xl * NZ + sender).wait_recv()
        dg_copy(1, z, (1 - xl) * NZ + sender).wait_recv()

    loop(1, NZ, dg_arrive)

    for step in range(NZ - 1):
        for way in range(2):
            ring_copy(way, step, ring_block(way, step)).wait_send()

    def row_sent(k):
        peer = lax.rem(r + k, R)
        mx_copy(peer, r).wait_send()
        dm_copy(peer, r).wait_send()

    loop(1, R, row_sent)

    def z_sent(k):
        peer = lax.rem(z + k, NZ)
        for n in range(2):
            gate_copy(n, peer, z).wait_send()
            dg_copy(n, peer, (r, pr)[n]).wait_send()

    loop(1, NZ, z_sent)

    def plane_sent(k):
        peer = lax.rem(f + k, F)
        for n in range(2):
            w_copy(n, peer, f).wait_send()
            gw_copy(n, peer, n * F + f).wait_send()
        gf_copy(peer, f).wait_send()

    loop(1, F, plane_sent)
    w_copy(1, f, f).wait_send()
    gw_copy(1, f, F + f).wait_send()
    conv_copy.wait_send()
    dconv_copy.wait_send()


def local(R, F, proj, dout, filt, w):
    proj, dout = proj.reshape(proj.shape[1:]), dout.reshape(dout.shape[1:])
    D = dout.shape[1]
    NZ = R // 2
    TB, CB, DB, PB = POS // R, D // R, D // F, POS // F
    tables = [jnp.asarray(t) for t in build_tables()]
    vmem = pl.BlockSpec(memory_space=pltpu.VMEM)
    hbm = pl.BlockSpec(memory_space=pl.ANY)
    dma = pltpu.SemaphoreType.DMA
    spectrum = pltpu.VMEM((LC + 2, LR, CB), F32)
    grads = pl.pallas_call(
        functools.partial(kernel, R, F, D),
        out_shape=(
            jax.ShapeDtypeStruct((TB, 3 * D), BF),
            jax.ShapeDtypeStruct((CB, DB), F32),
            jax.ShapeDtypeStruct((CB, PB), F32),
        ),
        in_specs=[
            hbm, hbm, hbm, vmem,
        ] + [vmem] * len(tables),
        out_specs=(vmem, vmem, vmem),
        scratch_shapes=[
            pltpu.VMEM((TB, D), BF), pltpu.VMEM((TB, D), BF),
            pltpu.VMEM((TB, D), BF),
            pltpu.VMEM((POS, CB), BF),
            pltpu.VMEM((2, HALF, CB), BF),
            pltpu.VMEM((2, HALF, CB), BF),
            pltpu.VMEM((HALF, CB), BF),
            pltpu.VMEM((HALF, D), BF),
            pltpu.VMEM((2 * CB, D), BF),
            spectrum, spectrum, spectrum,
            pltpu.VMEM((LC, LR, CB), F32),
            pltpu.VMEM((HALF // (G * LC), 2 * CB, G * LC), BF),
            pltpu.VMEM((HALF, CB), BF),
            pltpu.VMEM((POS, CB), BF),
            pltpu.VMEM((2, HALF, CB), BF),
            pltpu.VMEM((POS, CB), BF),
            pltpu.VMEM((TB, D), BF),
            pltpu.VMEM((F, 2, CB, DB), BF),
            pltpu.VMEM((2 * F, CB, DB), BF),
            pltpu.VMEM((POS, CB), BF),
            pltpu.VMEM((F, PB, CB), BF),
            dma((10,)),
            dma((2, NZ)), dma((2, NZ)),
            dma((R,)), dma((R,)),
            dma((2, NZ)), dma((2, NZ)),
            dma((2, F)), dma((2, F)),
            dma((2,)), dma((2,)),
            dma((2, NZ)), dma((R,)),
            dma((R,)), dma((R,)),
            dma((2, F)), dma((2 * F,)),
            dma((F,)), dma((F,)),
        ],
        compiler_params=pltpu.CompilerParams(
            collective_id=0, has_side_effects=True, vmem_limit_bytes=62 * 1024 * 1024
        ),
    )(proj, dout, w, filt, *tables)
    return grads[0][None], grads[1], grads[2]


def solution(mesh):
    placed = (P("frame", "row", None), P("frame", "row", None), P("row", None), P("row", "frame"))
    return jax.shard_map(
        functools.partial(local, mesh.shape["row"], mesh.shape["frame"]),
        mesh=mesh,
        in_specs=placed,
        out_specs=(P("frame", "row", None), P("row", "frame"), P("row", "frame")),
        check_vma=False,
    )
```

time: 494 us -> 237 us (0.48)
  Pallas kernels: 0 us -> 228 us
  waiting for transfers between devices: 169 us -> 0 us
  local copies, waits for them, and re-layouts: 105 us -> 5.25 us
  other arithmetic: 99.3 us -> 0 us
  matrix products: 65.8 us -> 0 us
  starting transfers between devices: 35 us -> 0 us
  between operations: 14.3 us -> 0.66 us
    pallas_call x0 -> x1, Pallas kernels: none -> 228 us  [local(): pl.pallas_call(functools.partial(kernel, R, F, D), out_shape=(jax.ShapeDt...]
    all_gather x2 -> x0, waiting for transfers between devices: 121 us -> none  [the longest x1 121 us: local(): piece = lax.all_gather(dout, 'row', axis=1, tiled=True)]
    unnamed x4 -> x0, other arithmetic: 69 us -> none
    dot_general x14 -> x0, matrix products: 65.8 us -> none  [the longest x3 15.7 us: forward_dft(): return jnp.einsum('qkpi,...piln->...qkln', row_fwd, part, precision=HIGH)]
    all_to_all x4 -> x0, waiting for transfers between devices: 41.9 us -> none  [the longest x1 23 us: local(): lax.all_to_all(mixed, 'row', split_axis=2, concat_axis=1, tiled=True)]
    unnamed x42 -> x7, local copies, waits for them, and re-layouts: 45.9 us -> 5.25 us
    all_to_all x4 -> x0, starting transfers between devices: 34.3 us -> none  [the longest x1 10.1 us: local(): lax.all_to_all(gate_b, 'row', split_axis=2, concat_axis=1, tiled=True)]
    convert_element_type x3 -> x0, local copies, waits for them, and re-layouts: 25.2 us -> none  [the longest x1 17 us: local(): (gate_a.astype(jnp.float32) * value.astype(jnp.float32)).astype(jnp.bfloa...]
  transfers between devices with their start and end apart: 8 -> 0, of which waited for: 4 -> 0; matrix products, arithmetic and copies ran while one was open for 49% -> 0% of each run, Pallas kernels for 0% -> 0%
where the time goes in v1:
time: 237 us; the launch traced here: 234 us
  Pallas kernels  228 us (96%)
  local copies, waits for them, and re-layouts  5.25 us (2%)
    pallas_call x1, Pallas kernels, local(): pl.pallas_call(functools.partial(kernel, R, F, D), out_shape=(jax.ShapeDt...  228 us
    unnamed x7, local copies, waits for them, and re-layouts  5.25 us

profile of v1, /device:TPU:32, one launch (start us, length us, event | category | flops | bytes accessed | tf_op | source)
XLA Modules:
  0.0 233.6 jit_solution(17825887922013271562)
XLA Ops:
  0.6 227.7 %shard_map.175 = (bf16[128,12288]{1,0:T(8,128)(2,1)}, f32[256,256]{1,0:T(8,128)}, f32[256,128]{1,0:T(8,128)}) custom-call(bf16[128,12288]{1,0:T(8,128)(2,1)} %bitcast.3, bf16[128,4096]{1,0:T(8,128)(2,1)} %bitcast.5, bf16[256,256]{1,0:T(8,128)(2,1)} %w.1, f32[256,2048]{1,0:T(8,128)} %filt.1, bf16[256,256]{1,0:T(8,128)(2,1)} %constant.24.clone.a1h, ...), custom_call_target="tpu_custom_call" | custom-call | tf_op jit(solution)/shard_map/pallas_call | solution.py:476
  228.4 0.0 copy-start
  228.4 0.0 copy-start.1
  228.4 3.9 %copy.22 = bf16[1,128,12288]{2,1,0:T(8,128)(2,1)} copy(bf16[1,128,12288]{2,1,0:T(8,128)(2,1)} %bitcast.4) | data formatting | bytes 6291456
  232.3 0.0 copy-done
  232.3 0.7 copy.23
  233.0 0.0 copy-done.1
  233.0 0.7 copy.24
Async XLA Ops:
  228.4 3.9 %copy-start = (f32[256,256]{1,0:T(8,128)S(1)}, f32[256,256]{1,0:T(8,128)}, u32[]{:S(2)}) copy-start(f32[256,256]{1,0:T(8,128)} %get-tuple-element.13) | copy-start | bytes 786436
  228.4 4.6 %copy-start.1 = (f32[256,128]{1,0:T(8,128)S(1)}, f32[256,128]{1,0:T(8,128)}, u32[]{:S(2)}) copy-start(f32[256,128]{1,0:T(8,128)} %get-tuple-element.14) | copy-start | bytes 393220

commit v2 on v1

--- a/solution.py
+++ b/solution.py
@@ -13,6 +13,8 @@
 LC = 32
 POS = LR * LC
 HALF = POS // 2
+RIGHT = 8
+SUB = 2
 G = 8
 MESH = pl.DeviceIdType.MESH
 BF = jnp.bfloat16
@@ -73,12 +75,14 @@
 
 
 def kernel(
-    R, F, D,
+    R, F, D, CR,
     proj, dout, w, filt,
     a1h, a1l, a2h, a2l, azh, azl, b2h, b2l, bzh, bzl, b1h, b1l,
     out, gw_out, gf_out,
-    value, gate_a, mx, mch, gmn, cmn, cvo, dh, w2, fsp, msp, dsp, tmp, gt, dcv, dch, dg, dms, dmt, gws, gwr, gfs, gfr,
-    local, ring_s, ring_r, mx_s, mx_r, gate_s, gate_r, w_s, w_r, x_s, x_r, dg_s, dg_r, dm_s, dm_r, gw_s, gw_r, gf_s, gf_r,
+    value, gate_a, mx, mch, gmn, cmn, cvo, dh, w2, fsp, msp, dsp, tmp, acc, gt, dcv, dch, dg, dms, dmt,
+    gwx, gwy, gws, gwr, gff, gfx, gfy, gfs, gfr,
+    local, ring_s, ring_r, mx_s, mx_r, gate_s, gate_r, w_s, w_r, x_s, x_r, dg_s, dg_r, dm_s, dm_r,
+    gwx_s, gwx_r, gw_s, gw_r, gfx_s, gfx_r, gf_s, gf_r,
 ):
     NZ = R // 2
     TB, CB, DB, PB = POS // R, D // R, D // F, POS // F
@@ -87,6 +91,9 @@
     pr = (1 - xl) * NZ + z
     right = xl * NZ + lax.rem(z + 1, NZ)
     left = xl * NZ + lax.rem(z + NZ - 1, NZ)
+    FC = F // 2
+    chip, core = lax.div(f, 2), lax.rem(f, 2)
+    twin = f + 1 - 2 * core
 
     def at(index, size):
         return pl.ds(pl.multiple_of(index * size, size), size)
@@ -140,21 +147,26 @@
     own_dout.wait()
     pl.semaphore_wait(barrier, (R - 1) + 2 * (F - 1))
 
-    def ring_copy(way, step, block):
-        rows = pl.ds(pl.multiple_of(block * TB + way * (TB // 2), TB // 2), TB // 2)
-        place = dh.at[rows, :]
-        return remote(place, place, ring_s.at[way, step], ring_r.at[way, step], f, (right, left)[way])
+    def ring_part(way, sub):
+        width = (CR if way == 0 else D - CR) // SUB
+        return pl.ds((0 if way == 0 else CR) + sub * width, width)
+
+    def ring_copy(way, sub, step, block):
+        place = dh.at[at(block, TB), ring_part(way, sub)]
+        n = way * SUB + sub
+        return remote(place, place, ring_s.at[n, step], ring_r.at[n, step], f, (right, left)[way])
 
     def ring_block(way, step):
         return lax.rem(z + NZ - step, NZ) if way == 0 else lax.rem(z + step, NZ)
 
     def ring(step):
         if step < NZ:
-            for way in range(2):
-                if step > 0:
-                    ring_copy(way, step - 1, ring_block(way, step)).wait_recv()
-                if step < NZ - 1:
-                    ring_copy(way, step, ring_block(way, step)).start()
+            for sub in range(SUB):
+                for way in range(2):
+                    if step > 0:
+                        ring_copy(way, sub, step - 1, ring_block(way, step)).wait_recv()
+                    if step < NZ - 1:
+                        ring_copy(way, sub, step, ring_block(way, step)).start()
 
     def mx_copy(peer, sender):
         return remote(mx.at[:, at(peer, CB)], mch.at[at(sender, TB), :], mx_s.at[peer], mx_r.at[sender], f, peer)
@@ -236,8 +248,8 @@
         columns(k, dot3(a1h[...], a1l[...], filt[:, at(k, CH)], dot_t))
 
     loop(0, CHUNKS, filt_step)
+    ring(1)
     rows_fwd(fsp)
-    ring(1)
 
     own_mx.wait()
 
@@ -265,20 +277,12 @@
         cvo[at(k, CH), :] = columns_inv((1 - xl) * (CHUNKS // 2) + k).astype(BF)
 
     loop(0, CHUNKS // 2, conv_step)
-    conv_copy = remote(cvo, cmn.at[1], x_s.at[0], x_r.at[0], f, pr)
+    conv_copy = remote(cvo, cmn.at[1], x_s.at[NZ], x_r.at[NZ], f, pr)
     conv_copy.start()
     for copy in own_gate:
         copy.wait()
     own_w.wait()
-    for step in range(4, NZ):
-        ring(step)
-
-    def wait_gate(k):
-        sender = lax.rem(z + NZ - k, NZ)
-        gate_copy(0, z, sender).wait_recv()
-        gate_copy(1, z, sender).wait_recv()
-
-    loop(1, NZ, wait_gate)
+    ring(4)
 
     def wait_w(k):
         sender = lax.rem(f + F - k, F)
@@ -287,46 +291,23 @@
 
     w_copy(1, f, f).wait_recv()
     loop(1, F, wait_w)
-    conv_copy.wait_recv()
-
-    def dgated_step(m):
-        rows = at(m, CH)
-        term = dot_t(dh[rows, :], w2[...])
-        for n in range(2):
-            d = term[:, n * CB : (n + 1) * CB]
-            gate = gmn[n, rows, :].astype(F32)
-            conv = cmn[n, rows, :].astype(F32)
-            gt[m, pl.ds(n * CB, CB), :] = (gate * conv).T.astype(BF)
-            dg[n, rows, :] = (d * conv).astype(BF)
-            dconv = (d * gate).astype(BF)
-            if n == 0:
-                dch[pl.ds(pl.multiple_of(xl * HALF + m * CH, CH), CH), :] = dconv
+
+    def part(t):
+        if t == 0:
+            acc[at(z, TB), :] = dot_t(dh[at(z, TB), :], w2[...])
+            return
+        for way in range(2):
+            rows = at(ring_block(way, t), TB)
+            cols = pl.ds(0, CR) if way == 0 else pl.ds(CR, D - CR)
+            term = dot_t(dh[rows, cols], w2[:, cols])
+            if t < NZ // 2 or (t == NZ // 2 and way == 0):
+                acc[rows, :] = term
             else:
-                dcv[rows, :] = dconv
-
-    loop(0, HALF // CH, dgated_step)
-    dconv_copy = remote(dcv, dch.at[at(xl, HALF), :], x_s.at[1], x_r.at[1], f, pr)
-    dconv_copy.start()
-
-    def gw_copy(n, peer, slot):
-        return remote(gws.at[peer, n], gwr.at[slot], gw_s.at[n, peer], gw_r.at[slot], peer, (r, pr)[n])
-
-    def gw_step(k):
-        peer = lax.rem(f + k, F)
-        total = jnp.zeros((2 * CB, DB), F32)
-        for m in range(HALF // CH):
-            total = total + dot(gt[m], dh[pl.ds(m * CH, CH), at(peer, DB)])
-        piece = total.astype(BF)
-        gws[peer, 0] = piece[:CB]
-        gws[peer, 1] = piece[CB:]
-        gw_copy(1, peer, F + f).start()
-
-    def gw_send_step(k):
-        gw_step(k)
-        gw_copy(0, lax.rem(f + k, F), f).start()
-
-    loop(1, F, gw_send_step)
-    gw_step(0)
+                acc[rows, :] += term
+
+    def dconv_copy(block, half):
+        rows = pl.ds(pl.multiple_of(half * HALF + block * TB, TB), TB)
+        return remote(dcv.at[at(block, TB), :], dch.at[rows, :], x_s.at[block], x_r.at[block], f, pr)
 
     def dg_copy(n, peer_z, channel):
         return remote(
@@ -338,17 +319,91 @@
         pltpu.make_async_copy(dg.at[n, at(z, TB), :], out.at[:, at(2 * R + c, CB)], local.at[5 + n])
         for n, c in enumerate((r, pr))
     ]
-    for copy in own_dg:
-        copy.start()
-
-    def send_dg(k):
-        peer = lax.rem(z + k, NZ)
-        dg_copy(0, peer, r).start()
-        dg_copy(1, peer, pr).start()
-
-    loop(1, NZ, send_dg)
-
-    dconv_copy.wait_recv()
+
+    def finalize(block, own):
+        rows = at(block, TB)
+        for n in range(2):
+            d = acc[rows, n * CB : (n + 1) * CB]
+            gate = gmn[n, rows, :].astype(F32)
+            conv = cmn[n, rows, :].astype(F32)
+            gt[n * CB : (n + 1) * CB, rows] = (gate * conv).T.astype(BF)
+            dg[n, rows, :] = (d * conv).astype(BF)
+            dconv = (d * gate).astype(BF)
+            if n == 0:
+                dch[pl.ds(pl.multiple_of(xl * HALF + block * TB, TB), TB), :] = dconv
+            else:
+                dcv[rows, :] = dconv
+        dconv_copy(block, xl).start()
+        if own:
+            for copy in own_dg:
+                copy.start()
+        else:
+            dg_copy(0, block, r).start()
+            dg_copy(1, block, pr).start()
+
+    def wait_gate(k):
+        sender = lax.rem(z + NZ - k, NZ)
+        gate_copy(0, z, sender).wait_recv()
+        gate_copy(1, z, sender).wait_recv()
+
+    def step_done(t):
+        part(t)
+        if t == 0:
+            finalize(z, True)
+        elif t == NZ // 2:
+            finalize(ring_block(0, t), False)
+        elif t > NZ // 2:
+            finalize(ring_block(0, t), False)
+            finalize(ring_block(1, t), False)
+
+    for t in range(1, min(4, NZ)):
+        part(t)
+    loop(1, NZ, wait_gate)
+    conv_copy.wait_recv()
+    step_done(0)
+    if NZ <= 4:
+        for t in range(NZ // 2, NZ):
+            finalize(ring_block(0, t), False)
+            if t > NZ // 2:
+                finalize(ring_block(1, t), False)
+    ring(5)
+    for t in range(4, NZ):
+        step_done(t)
+        ring(t + 2)
+
+    def gw_partial(cols):
+        return dot(gt[...], dh[:, at(cols, DB)])
+
+    def gwx_copy(j):
+        return remote(gwx.at[j], gwy.at[j], gwx_s.at[j], gwx_r.at[j], twin, r)
+
+    def gwx_step(k):
+        j = lax.rem(chip + k, FC)
+        gwx[j] = gw_partial(2 * j + 1 - core).astype(BF)
+        gwx_copy(j).start()
+
+    loop(0, FC, gwx_step)
+
+    def gw_copy(n, peer, sender):
+        return remote(gws.at[peer, n], gwr.at[n, sender], gw_s.at[n, peer], gw_r.at[n, sender], 2 * peer + core, (r, pr)[n])
+
+    def gw_step(j):
+        total = gw_partial(2 * j + core)
+        gwx_copy(j).wait_recv()
+        piece = (total + gwy[j].astype(F32)).astype(BF)
+        gws[j, 0] = piece[:CB]
+        gws[j, 1] = piece[CB:]
+        gw_copy(1, j, chip).start()
+
+    def gw_send_step(k):
+        j = lax.rem(chip + k, FC)
+        gw_step(j)
+        gw_copy(0, j, chip).start()
+
+    loop(1, FC, gw_send_step)
+    gw_step(chip)
+
+    loop(0, NZ, lambda k: dconv_copy(k, 1 - xl).wait_recv())
     loop(0, CHUNKS, plane_step(dch))
     rows_fwd(dsp)
     rows_inv(dsp, fsp, True)
@@ -368,14 +423,33 @@
     rows_inv(dsp, msp, True)
 
     def gf_step(k):
-        gfs[at(k, CH), :] = columns_inv(k).astype(BF)
+        gff[at(k, CH), :] = columns_inv(k)
 
     loop(0, CHUNKS, gf_step)
 
+    def gfx_copy(j):
+        return remote(gfx.at[j], gfy.at[j], gfx_s.at[j], gfx_r.at[j], twin, r)
+
+    def gfx_step(j):
+        gfx[j] = gff[at(2 * j + 1 - core, PB), :].astype(BF)
+        gfx_copy(j).start()
+
+    loop(0, FC, gfx_step)
+
     def gf_copy(peer, sender):
-        return remote(gfs.at[at(peer, PB), :], gfr.at[sender], gf_s.at[peer], gf_r.at[sender], peer, r)
-
-    loop(1, F, lambda k: gf_copy(lax.rem(f + k, F), f).start())
+        return remote(gfs.at[peer], gfr.at[sender], gf_s.at[peer], gf_r.at[sender], 2 * peer + core, r)
+
+    def gf_sum(j):
+        gfx_copy(j).wait_recv()
+        gfs[j] = (gff[at(2 * j + core, PB), :] + gfy[j].astype(F32)).astype(BF)
+
+    def gf_send_step(k):
+        j = lax.rem(chip + k, FC)
+        gf_sum(j)
+        gf_copy(j, chip).start()
+
+    loop(1, FC, gf_send_step)
+    gf_sum(chip)
 
     def finish(c):
         cols = at(c, CB)
@@ -393,30 +467,25 @@
 
     loop(1, R, dm_step)
 
-    gw_out[...] = gws[f, 0].astype(F32)
-
-    def gw_other(sender):
-        gw_copy(1, f, F + sender).wait_recv()
-        gw_out[...] += gwr[F + sender].astype(F32)
+    gw_out[...] = gws[chip, 0].astype(F32)
+
+    def gw_add(n, sender):
+        gw_copy(n, chip, sender).wait_recv()
+        gw_out[...] += gwr[n, sender].astype(F32)
 
     def gw_arrive(k):
-        sender = lax.rem(f + F - k, F)
-        gw_copy(0, f, sender).wait_recv()
-        gw_out[...] += gwr[sender].astype(F32)
-        gw_other(sender)
-
-    loop(1, F, gw_arrive)
-    gw_other(f)
+        sender = lax.rem(chip + FC - k, FC)
+        gw_add(0, sender)
+        gw_add(1, sender)
+
+    loop(1, FC, gw_arrive)
+    gw_add(1, chip)
     gw_out[...] = gw_out[...] * (1.0 / F)
 
-    gfr[f] = gfs[at(f, PB), :]
-
-    def gf_arrive(k):
-        gf_copy(f, lax.rem(f + F - k, F)).wait_recv()
-
-    loop(1, F, gf_arrive)
+    gfr[chip] = gfs[chip]
+    loop(1, FC, lambda k: gf_copy(chip, lax.rem(chip + FC - k, FC)).wait_recv())
     total = gfr[0].astype(F32)
-    for n in range(1, F):
+    for n in range(1, FC):
         total = total + gfr[n].astype(F32)
     gf_out[...] = total.T * (1.0 / F)
 
@@ -432,7 +501,8 @@
 
     for step in range(NZ - 1):
         for way in range(2):
-            ring_copy(way, step, ring_block(way, step)).wait_send()
+            for sub in range(SUB):
+                ring_copy(way, sub, step, ring_block(way, step)).wait_send()
 
     def row_sent(k):
         peer = lax.rem(r + k, R)
@@ -448,19 +518,30 @@
             dg_copy(n, peer, (r, pr)[n]).wait_send()
 
     loop(1, NZ, z_sent)
+    loop(0, NZ, lambda k: dconv_copy(k, xl).wait_send())
 
     def plane_sent(k):
         peer = lax.rem(f + k, F)
         for n in range(2):
             w_copy(n, peer, f).wait_send()
-            gw_copy(n, peer, n * F + f).wait_send()
-        gf_copy(peer, f).wait_send()
 
     loop(1, F, plane_sent)
+
+    def chip_sent(k):
+        peer = lax.rem(chip + k, FC)
+        gw_copy(0, peer, chip).wait_send()
+        gf_copy(peer, chip).wait_send()
+
+    loop(1, FC, chip_sent)
+
+    def twin_sent(j):
+        gw_copy(1, j, chip).wait_send()
+        gwx_copy(j).wait_send()
+        gfx_copy(j).wait_send()
+
+    loop(0, FC, twin_sent)
     w_copy(1, f, f).wait_send()
-    gw_copy(1, f, F + f).wait_send()
     conv_copy.wait_send()
-    dconv_copy.wait_send()
 
 
 def local(R, F, proj, dout, filt, w):
@@ -468,13 +549,14 @@
     D = dout.shape[1]
     NZ = R // 2
     TB, CB, DB, PB = POS // R, D // R, D // F, POS // F
+    CR = D * RIGHT // 16 // (128 * SUB) * (128 * SUB)
     tables = [jnp.asarray(t) for t in build_tables()]
     vmem = pl.BlockSpec(memory_space=pltpu.VMEM)
     hbm = pl.BlockSpec(memory_space=pl.ANY)
     dma = pltpu.SemaphoreType.DMA
     spectrum = pltpu.VMEM((LC + 2, LR, CB), F32)
     grads = pl.pallas_call(
-        functools.partial(kernel, R, F, D),
+        functools.partial(kernel, R, F, D, CR),
         out_shape=(
             jax.ShapeDtypeStruct((TB, 3 * D), BF),
             jax.ShapeDtypeStruct((CB, DB), F32),
@@ -495,26 +577,28 @@
             pltpu.VMEM((2 * CB, D), BF),
             spectrum, spectrum, spectrum,
             pltpu.VMEM((LC, LR, CB), F32),
-            pltpu.VMEM((HALF // (G * LC), 2 * CB, G * LC), BF),
+            pltpu.VMEM((HALF, 2 * CB), F32),
+            pltpu.VMEM((2 * CB, HALF), BF),
             pltpu.VMEM((HALF, CB), BF),
             pltpu.VMEM((POS, CB), BF),
             pltpu.VMEM((2, HALF, CB), BF),
             pltpu.VMEM((POS, CB), BF),
             pltpu.VMEM((TB, D), BF),
-            pltpu.VMEM((F, 2, CB, DB), BF),
-            pltpu.VMEM((2 * F, CB, DB), BF),
-            pltpu.VMEM((POS, CB), BF),
-            pltpu.VMEM((F, PB, CB), BF),
+            pltpu.VMEM((F // 2, 2 * CB, DB), BF), pltpu.VMEM((F // 2, 2 * CB, DB), BF),
+            pltpu.VMEM((F // 2, 2, CB, DB), BF), pltpu.VMEM((2, F // 2, CB, DB), BF),
+            pltpu.VMEM((POS, CB), F32),
+            pltpu.VMEM((F // 2, PB, CB), BF), pltpu.VMEM((F // 2, PB, CB), BF),
+            pltpu.VMEM((F // 2, PB, CB), BF), pltpu.VMEM((F // 2, PB, CB), BF),
             dma((10,)),
-            dma((2, NZ)), dma((2, NZ)),
+            dma((2 * SUB, NZ)), dma((2 * SUB, NZ)),
             dma((R,)), dma((R,)),
             dma((2, NZ)), dma((2, NZ)),
             dma((2, F)), dma((2, F)),
-            dma((2,)), dma((2,)),
+            dma((NZ + 1,)), dma((NZ + 1,)),
             dma((2, NZ)), dma((R,)),
             dma((R,)), dma((R,)),
-            dma((2, F)), dma((2 * F,)),
-            dma((F,)), dma((F,)),
+            dma((F // 2,)), dma((F // 2,)), dma((2, F // 2)), dma((2, F // 2)),
+            dma((F // 2,)), dma((F // 2,)), dma((F // 2,)), dma((F // 2,)),
         ],
         compiler_params=pltpu.CompilerParams(
             collective_id=0, has_side_effects=True, vmem_limit_bytes=62 * 1024 * 1024

time: 237 us -> 210 us (0.89)
  Pallas kernels: 228 us -> 200 us
    pallas_call x1, Pallas kernels: 228 us -> 200 us  [local(): pl.pallas_call(functools.partial(kernel, R, F, D, CR), out_shape=(jax.Sha...]
where the time goes in v2:
time: 210 us; the launch traced here: 206 us
  Pallas kernels  200 us (95%)
  local copies, waits for them, and re-layouts  5.25 us (2%)
    pallas_call x1, Pallas kernels, local(): pl.pallas_call(functools.partial(kernel, R, F, D, CR), out_shape=(jax.Sha...  200 us
    unnamed x7, local copies, waits for them, and re-layouts  5.25 us

profile of v2, /device:TPU:32, one launch (start us, length us, event | category | flops | bytes accessed | tf_op | source)
XLA Modules:
  0.0 206.4 jit_solution(11581872946184862678)
XLA Ops:
  0.6 200.5 %shard_map.175 = (bf16[128,12288]{1,0:T(8,128)(2,1)}, f32[256,256]{1,0:T(8,128)}, f32[256,128]{1,0:T(8,128)}) custom-call(bf16[128,12288]{1,0:T(8,128)(2,1)} %bitcast.3, bf16[128,4096]{1,0:T(8,128)(2,1)} %bitcast.5, bf16[256,256]{1,0:T(8,128)(2,1)} %w.1, f32[256,2048]{1,0:T(8,128)} %filt.1, bf16[256,256]{1,0:T(8,128)(2,1)} %constant.24.clone.a1h, ...), custom_call_target="tpu_custom_call" | custom-call | tf_op jit(solution)/shard_map/pallas_call | solution.py:558
  201.1 0.0 copy-start
  201.1 0.0 copy-start.1
  201.1 3.9 %copy.22 = bf16[1,128,12288]{2,1,0:T(8,128)(2,1)} copy(bf16[1,128,12288]{2,1,0:T(8,128)(2,1)} %bitcast.4) | data formatting | bytes 6291456
  205.0 0.0 copy-done
  205.0 0.7 copy.23
  205.7 0.0 copy-done.1
  205.7 0.7 copy.24
Async XLA Ops:
  201.1 3.9 %copy-start = (f32[256,256]{1,0:T(8,128)S(1)}, f32[256,256]{1,0:T(8,128)}, u32[]{:S(2)}) copy-start(f32[256,256]{1,0:T(8,128)} %get-tuple-element.13) | copy-start | bytes 786436
  201.1 4.6 %copy-start.1 = (f32[256,128]{1,0:T(8,128)S(1)}, f32[256,128]{1,0:T(8,128)}, u32[]{:S(2)}) copy-start(f32[256,128]{1,0:T(8,128)} %get-tuple-element.14) | copy-start | bytes 393220

commit v3 on v2

--- a/solution.py
+++ b/solution.py
@@ -76,10 +76,10 @@
 
 def kernel(
     R, F, D, CR,
-    proj, dout, w, filt,
-    a1h, a1l, a2h, a2l, azh, azl, b2h, b2l, bzh, bzl, b1h, b1l,
-    out, gw_out, gf_out,
-    value, gate_a, mx, mch, gmn, cmn, cvo, dh, w2, fsp, msp, dsp, tmp, acc, gt, dcv, dch, dg, dms, dmt,
+    proj, dout, w, filt_hbm, t0, t1, t2, t3, t4, t5, t6, t7, t8, t9, t10, t11,
+    dmt, dgt, gw_out, gf_out,
+    filt, a1h, a1l, a2h, a2l, azh, azl, b2h, b2l, bzh, bzl, b1h, b1l,
+    value, gate_a, mx, mch, gmn, cmn, cvo, dh, w2, fsp, msp, dsp, tmp, acc, gt, dcv, dch, dg, dms,
     gwx, gwy, gws, gwr, gff, gfx, gfy, gfs, gfr,
     local, ring_s, ring_r, mx_s, mx_r, gate_s, gate_r, w_s, w_r, x_s, x_r, dg_s, dg_r, dm_s, dm_r,
     gwx_s, gwx_r, gw_s, gw_r, gfx_s, gfx_r, gf_s, gf_r,
@@ -111,6 +111,19 @@
 
         lax.fori_loop(start, stop, body, 0)
 
+    barrier = pltpu.get_barrier_semaphore()
+
+    def greet(frame, row):
+        pl.semaphore_signal(barrier, inc=1, device_id={"frame": frame, "row": row}, device_id_type=MESH)
+
+    loop(1, R, lambda k: greet(f, lax.rem(r + k, R)))
+
+    def greet_plane(k):
+        greet(lax.rem(f + k, F), r)
+        greet(lax.rem(f + k, F), pr)
+
+    loop(1, F, greet_plane)
+
     own_dout = pltpu.make_async_copy(dout, dh.at[at(z, TB), :], local.at[0])
     own_w = pltpu.make_async_copy(w, w2.at[pl.ds(0, CB), at(f, DB)], local.at[1])
     own_gate = [
@@ -125,26 +138,23 @@
     own_w.start()
     for copy in own_gate:
         copy.start()
-
-    barrier = pltpu.get_barrier_semaphore()
-
-    def greet(frame, row):
-        pl.semaphore_signal(barrier, inc=1, device_id={"frame": frame, "row": row}, device_id_type=MESH)
-
-    loop(1, R, lambda k: greet(f, lax.rem(r + k, R)))
-
-    def greet_plane(k):
-        greet(lax.rem(f + k, F), r)
-        greet(lax.rem(f + k, F), pr)
-
-    loop(1, F, greet_plane)
+    own_tables = [
+        pltpu.make_async_copy(pair[0], pair[1], local.at[10 + n])
+        for n, pair in enumerate(
+            zip(
+                (filt_hbm, t0, t1, t2, t3, t4, t5, t6, t7, t8, t9, t10, t11),
+                (filt, a1h, a1l, a2h, a2l, azh, azl, b2h, b2l, bzh, bzl, b1h, b1l),
+            )
+        )
+    ]
+    for copy in own_tables:
+        copy.start()
 
     own_value.wait()
     own_a.wait()
     mx[...] = (value[...].astype(F32) * gate_a[...].astype(F32)).astype(BF)
     own_mx = pltpu.make_async_copy(mx.at[:, at(r, CB)], mch.at[at(r, TB), :], local.at[4])
     own_mx.start()
-    own_dout.wait()
     pl.semaphore_wait(barrier, (R - 1) + 2 * (F - 1))
 
     def ring_part(way, sub):
@@ -154,7 +164,8 @@
     def ring_copy(way, sub, step, block):
         place = dh.at[at(block, TB), ring_part(way, sub)]
         n = way * SUB + sub
-        return remote(place, place, ring_s.at[n, step], ring_r.at[n, step], f, (right, left)[way])
+        first = dout.at[:, ring_part(way, sub)] if step == 0 else place
+        return remote(first, place, ring_s.at[n, step], ring_r.at[n, step], f, (right, left)[way])
 
     def ring_block(way, step):
         return lax.rem(z + NZ - step, NZ) if way == 0 else lax.rem(z + step, NZ)
@@ -247,6 +258,8 @@
     def filt_step(k):
         columns(k, dot3(a1h[...], a1l[...], filt[:, at(k, CH)], dot_t))
 
+    for copy in own_tables:
+        copy.wait()
     loop(0, CHUNKS, filt_step)
     ring(1)
     rows_fwd(fsp)
@@ -282,6 +295,7 @@
     for copy in own_gate:
         copy.wait()
     own_w.wait()
+    own_dout.wait()
     ring(4)
 
     def wait_w(k):
@@ -311,16 +325,16 @@
 
     def dg_copy(n, peer_z, channel):
         return remote(
-            dg.at[n, at(peer_z, TB), :], out.at[:, at(2 * R + channel, CB)],
+            dg.at[n, at(peer_z, TB), :], dgt.at[:, at(channel, CB)],
             dg_s.at[n, peer_z], dg_r.at[channel], f, xl * NZ + peer_z,
         )
 
     own_dg = [
-        pltpu.make_async_copy(dg.at[n, at(z, TB), :], out.at[:, at(2 * R + c, CB)], local.at[5 + n])
+        pltpu.make_async_copy(dg.at[n, at(z, TB), :], dgt.at[:, at(c, CB)], local.at[5 + n])
         for n, c in enumerate((r, pr))
     ]
 
-    def finalize(block, own):
+    def finalize(block):
         rows = at(block, TB)
         for n in range(2):
             d = acc[rows, n * CB : (n + 1) * CB]
@@ -334,12 +348,6 @@
             else:
                 dcv[rows, :] = dconv
         dconv_copy(block, xl).start()
-        if own:
-            for copy in own_dg:
-                copy.start()
-        else:
-            dg_copy(0, block, r).start()
-            dg_copy(1, block, pr).start()
 
     def wait_gate(k):
         sender = lax.rem(z + NZ - k, NZ)
@@ -349,12 +357,12 @@
     def step_done(t):
         part(t)
         if t == 0:
-            finalize(z, True)
+            finalize(z)
         elif t == NZ // 2:
-            finalize(ring_block(0, t), False)
+            finalize(ring_block(0, t))
         elif t > NZ // 2:
-            finalize(ring_block(0, t), False)
-            finalize(ring_block(1, t), False)
+            finalize(ring_block(0, t))
+            finalize(ring_block(1, t))
 
     for t in range(1, min(4, NZ)):
         part(t)
@@ -363,13 +371,27 @@
     step_done(0)
     if NZ <= 4:
         for t in range(NZ // 2, NZ):
-            finalize(ring_block(0, t), False)
+            finalize(ring_block(0, t))
             if t > NZ // 2:
-                finalize(ring_block(1, t), False)
+                finalize(ring_block(1, t))
     ring(5)
+    def send_dg(k):
+        peer = lax.rem(z + k, NZ)
+        dg_copy(0, peer, r).start()
+        dg_copy(1, peer, pr).start()
+
     for t in range(4, NZ):
+        if t == NZ - 1:
+            loop(2, NZ - 1, send_dg)
         step_done(t)
         ring(t + 2)
+    if NZ <= 4:
+        loop(2, NZ - 1, send_dg)
+    send_dg(1)
+    if NZ > 2:
+        send_dg(NZ - 1)
+    for copy in own_dg:
+        copy.start()
 
     def gw_partial(cols):
         return dot(gt[...], dh[:, at(cols, DB)])
@@ -408,15 +430,21 @@
     rows_fwd(dsp)
     rows_inv(dsp, fsp, True)
 
-    def dmixed_step(k):
-        dms[at(k, CH), :] = columns_inv(k).astype(BF)
-
-    loop(0, CHUNKS, dmixed_step)
-
     def dm_copy(peer, sender):
         return remote(dms.at[at(peer, TB), :], dmt.at[:, at(sender, CB)], dm_s.at[peer], dm_r.at[sender], f, peer)
 
-    loop(1, R, lambda k: dm_copy(lax.rem(r + k, R), r).start())
+    def dm_send(peer):
+        @pl.when(peer != r)
+        def _():
+            dm_copy(peer, r).start()
+
+    def dmixed_step(k):
+        chunk = lax.rem(lax.div(r * TB, CH) + 1 + k, CHUNKS)
+        dms[at(chunk, CH), :] = columns_inv(chunk).astype(BF)
+        for n in range(CH // TB):
+            dm_send(chunk * (CH // TB) + n)
+
+    loop(0, CHUNKS, dmixed_step)
     own_dm = pltpu.make_async_copy(dms.at[at(r, TB), :], dmt.at[:, at(r, CB)], local.at[7])
     own_dm.start()
 
@@ -450,22 +478,6 @@
 
     loop(1, FC, gf_send_step)
     gf_sum(chip)
-
-    def finish(c):
-        cols = at(c, CB)
-        d = dmt[:, cols].astype(F32)
-        out[:, cols] = (d * gate_a[:, cols].astype(F32)).astype(BF)
-        out[:, at(R + c, CB)] = (d * value[:, cols].astype(F32)).astype(BF)
-
-    own_dm.wait()
-    finish(r)
-
-    def dm_step(k):
-        sender = lax.rem(r + R - k, R)
-        dm_copy(r, sender).wait_recv()
-        finish(sender)
-
-    loop(1, R, dm_step)
 
     gw_out[...] = gws[chip, 0].astype(F32)
 
@@ -499,6 +511,9 @@
 
     loop(1, NZ, dg_arrive)
 
+    own_dm.wait()
+    loop(1, R, lambda k: dm_copy(r, lax.rem(r + R - k, R)).wait_recv())
+
     for step in range(NZ - 1):
         for way in range(2):
             for sub in range(SUB):
@@ -542,6 +557,19 @@
     loop(0, FC, twin_sent)
     w_copy(1, f, f).wait_send()
     conv_copy.wait_send()
+
+
+def finish(value, gate_a, dmixed, dgate, gw, gf, out, gw_out, gf_out):
+    D = dmixed.shape[1]
+    d = dmixed[...].astype(F32)
+    out[:, :D] = (d * gate_a[...].astype(F32)).astype(BF)
+    out[:, D : 2 * D] = (d * value[...].astype(F32)).astype(BF)
+    out[:, 2 * D :] = dgate[...]
+
+    @pl.when(pl.program_id(0) == 0)
+    def _():
+        gw_out[...] = gw[...]
+        gf_out[...] = gf[...]
 
 
 def local(R, F, proj, dout, filt, w):
@@ -558,15 +586,18 @@
     grads = pl.pallas_call(
         functools.partial(kernel, R, F, D, CR),
         out_shape=(
-            jax.ShapeDtypeStruct((TB, 3 * D), BF),
+            jax.ShapeDtypeStruct((TB, D), BF),
+            jax.ShapeDtypeStruct((TB, D), BF),
             jax.ShapeDtypeStruct((CB, DB), F32),
             jax.ShapeDtypeStruct((CB, PB), F32),
         ),
         in_specs=[
-            hbm, hbm, hbm, vmem,
-        ] + [vmem] * len(tables),
-        out_specs=(vmem, vmem, vmem),
+            hbm, hbm, hbm, hbm,
+        ] + [hbm] * len(tables),
+        out_specs=(hbm, hbm, vmem, vmem),
         scratch_shapes=[
+            pltpu.VMEM((CB, POS), F32),
+        ] + [pltpu.VMEM(t.shape, BF) for t in tables] + [
             pltpu.VMEM((TB, D), BF), pltpu.VMEM((TB, D), BF),
             pltpu.VMEM((TB, D), BF),
             pltpu.VMEM((POS, CB), BF),
@@ -583,13 +614,12 @@
             pltpu.VMEM((POS, CB), BF),
             pltpu.VMEM((2, HALF, CB), BF),
             pltpu.VMEM((POS, CB), BF),
-            pltpu.VMEM((TB, D), BF),
             pltpu.VMEM((F // 2, 2 * CB, DB), BF), pltpu.VMEM((F // 2, 2 * CB, DB), BF),
             pltpu.VMEM((F // 2, 2, CB, DB), BF), pltpu.VMEM((2, F // 2, CB, DB), BF),
             pltpu.VMEM((POS, CB), F32),
             pltpu.VMEM((F // 2, PB, CB), BF), pltpu.VMEM((F // 2, PB, CB), BF),
             pltpu.VMEM((F // 2, PB, CB), BF), pltpu.VMEM((F // 2, PB, CB), BF),
-            dma((10,)),
+            dma((23,)),
             dma((2 * SUB, NZ)), dma((2 * SUB, NZ)),
             dma((R,)), dma((R,)),
             dma((2, NZ)), dma((2, NZ)),
@@ -604,7 +634,28 @@
             collective_id=0, has_side_effects=True, vmem_limit_bytes=62 * 1024 * 1024
         ),
     )(proj, dout, w, filt, *tables)
-    return grads[0][None], grads[1], grads[2]
+    dmixed, dgate, gw, gf = grads
+    rows = TB // 2
+    whole = lambda *shape: pl.BlockSpec(shape, lambda i: (0, 0))
+    grad_proj, gw, gf = pl.pallas_call(
+        finish,
+        grid=(TB // rows,),
+        out_shape=(
+            jax.ShapeDtypeStruct((TB, 3 * D), BF),
+            jax.ShapeDtypeStruct((CB, DB), F32),
+            jax.ShapeDtypeStruct((CB, PB), F32),
+        ),
+        in_specs=[
+            pl.BlockSpec((rows, D), lambda i: (i, 0)),
+            pl.BlockSpec((rows, D), lambda i: (i, 1)),
+            pl.BlockSpec((rows, D), lambda i: (i, 0)),
+            pl.BlockSpec((rows, D), lambda i: (i, 0)),
+            whole(CB, DB),
+            whole(CB, PB),
+        ],
+        out_specs=(pl.BlockSpec((rows, 3 * D), lambda i: (i, 0)), whole(CB, DB), whole(CB, PB)),
+    )(proj, proj, dmixed, dgate, gw, gf)
+    return grad_proj[None], gw, gf
 
 
 def solution(mesh):

time: 210 us -> 197 us (0.938)
  Pallas kernels: 200 us -> 193 us
  local copies, waits for them, and re-layouts: 5.25 us -> 0 us
    pallas_call x1, Pallas kernels: 200 us -> 190 us  [local(): pl.pallas_call(functools.partial(kernel, R, F, D, CR), out_shape=(jax.Sha...]
    unnamed x7 -> x0, local copies, waits for them, and re-layouts: 5.25 us -> none
    pallas_call x0 -> x1, Pallas kernels: none -> 3.85 us  [local(): pl.pallas_call(finish, grid=(TB // rows,), out_shape=(jax.ShapeDtypeStruc...]
where the time goes in v3:
time: 197 us; the launch traced here: 194 us
  Pallas kernels  193 us (98%)
    pallas_call x1, Pallas kernels, local(): pl.pallas_call(functools.partial(kernel, R, F, D, CR), out_shape=(jax.Sha...  190 us

profile of v3, /device:TPU:32, one launch (start us, length us, event | category | flops | bytes accessed | tf_op | source)
XLA Modules:
  0.0 194.1 jit_solution(1696829459213157161)
XLA Ops:
  0.6 189.6 %shard_map.175 = (bf16[128,4096]{1,0:T(8,128)(2,1)}, bf16[128,4096]{1,0:T(8,128)(2,1)}, f32[256,256]{1,0:T(8,128)}, f32[256,128]{1,0:T(8,128)}) custom-call(bf16[128,12288]{1,0:T(8,128)(2,1)} %bitcast.3, bf16[128,4096]{1,0:T(8,128)(2,1)} %bitcast.6, bf16[256,256]{1,0:T(8,128)(2,1)} %w.1, f32[256,2048]{1,0:T(8,128)} %filt_hbm.1, ...), custom_call_target="tpu_custom_call" | custom-call | tf_op jit(solution)/shard_map/pallas_call | solution.py:586
  190.2 3.9 %shard_map.176 = (bf16[128,12288]{1,0:T(8,128)(2,1)}, f32[256,256]{1,0:T(8,128)}, f32[256,128]{1,0:T(8,128)}) custom-call(bf16[128,12288]{1,0:T(8,128)(2,1)} %bitcast.4, bf16[128,12288]{1,0:T(8,128)(2,1)} %bitcast.5, bf16[128,4096]{1,0:T(8,128)(2,1)} %get-tuple-element.10.dmixed, bf16[128,4096]{1,0:T(8,128)(2,1)} %get-tuple-element.11.dgate, ...), custom_call_target="tpu_custom_call" | custom-call | tf_op jit(solution)/shard_map/pallas_call | solution.py:640

commit v4 on v3

--- a/solution.py
+++ b/solution.py
@@ -15,6 +15,8 @@
 HALF = POS // 2
 RIGHT = 8
 SUB = 2
+ROWS = 5
+COLS = 4
 G = 8
 MESH = pl.DeviceIdType.MESH
 BF = jnp.bfloat16
@@ -80,9 +82,9 @@
     dmt, dgt, gw_out, gf_out,
     filt, a1h, a1l, a2h, a2l, azh, azl, b2h, b2l, bzh, bzl, b1h, b1l,
     value, gate_a, mx, mch, gmn, cmn, cvo, dh, w2, fsp, msp, dsp, tmp, acc, gt, dcv, dch, dg, dms,
-    gwx, gwy, gws, gwr, gff, gfx, gfy, gfs, gfr,
+    gwx, gwy, gws, gwr, gwp, gwq, gff, gfx, gfy, gfs, gfr,
     local, ring_s, ring_r, mx_s, mx_r, gate_s, gate_r, w_s, w_r, x_s, x_r, dg_s, dg_r, dm_s, dm_r,
-    gwx_s, gwx_r, gw_s, gw_r, gfx_s, gfx_r, gf_s, gf_r,
+    gwx_s, gwx_r, gw_s, gw_r, gwz_s, gwz_r, gfx_s, gfx_r, gf_s, gf_r,
 ):
     NZ = R // 2
     TB, CB, DB, PB = POS // R, D // R, D // F, POS // F
@@ -94,6 +96,9 @@
     FC = F // 2
     chip, core = lax.div(f, 2), lax.rem(f, 2)
     twin = f + 1 - 2 * core
+    NX = 2 if F >= 8 else 1
+    NY = FC // NX
+    xh, y = lax.div(chip, NY), lax.rem(chip, NY)
 
     def at(index, size):
         return pl.ds(pl.multiple_of(index * size, size), size)
@@ -104,12 +109,12 @@
             device_id={"frame": frame, "row": row}, device_id_type=MESH,
         )
 
-    def loop(start, stop, step):
+    def loop(start, stop, step, unroll=1):
         def body(k, carry):
             step(k)
             return carry
 
-        lax.fori_loop(start, stop, body, 0)
+        lax.fori_loop(start, stop, body, 0, unroll=unroll)
 
     barrier = pltpu.get_barrier_semaphore()
 
@@ -230,24 +235,36 @@
         def step(l):
             dst[pl.ds(2 * l, 2)] = dot3(a2h[...], a2l[...], pair(tmp, 2 * l)).reshape(2, LR, CB)
 
-        loop(1, LC // 2, step)
-
-    def multiply(a, b, index, conjugate):
-        are, aim, bre, bim = a[index], a[index + 1], b[index], b[index + 1]
+        loop(1, LC // 2, step, ROWS)
+
+    def multiply(a, b, conjugate):
+        are, aim, bre, bim = a[0], a[1], b[0], b[1]
         if conjugate:
-            return are * bre + aim * bim, aim * bre - are * bim
-        return are * bre - aim * bim, are * bim + aim * bre
-
-    def rows_inv(a, b, conjugate):
-        first, last = multiply(a, b, 0, conjugate), multiply(a, b, LC, conjugate)
-        edge = jnp.concatenate(first + last, axis=0)
+            both = are * bre + aim * bim, aim * bre - are * bim
+        else:
+            both = are * bre - aim * bim, are * bim + aim * bre
+        return jnp.concatenate(both, axis=0)
+
+    def rows_product(a, b, conjugate, forward):
+        if forward:
+            edge = dot3(azh[...], azl[...], pair(tmp, 0)).reshape(4, LR, CB)
+            a[0:2] = edge[0:2]
+            a[LC : LC + 2] = edge[2:4]
+        else:
+            edge = jnp.concatenate((a[0:2], a[LC : LC + 2]), axis=0)
+        edge = jnp.concatenate((multiply(edge[0:2], b[0:2], conjugate), multiply(edge[2:4], b[LC : LC + 2], conjugate)), axis=0)
         tmp[0:2] = dot3(bzh[...], bzl[...], edge).reshape(2, LR, CB)
 
         def step(l):
-            both = jnp.concatenate(multiply(a, b, 2 * l, conjugate), axis=0)
-            tmp[pl.ds(2 * l, 2)] = dot3(b2h[...], b2l[...], both).reshape(2, LR, CB)
-
-        loop(1, LC // 2, step)
+            place = pl.ds(2 * l, 2)
+            if forward:
+                spectrum = dot3(a2h[...], a2l[...], pair(tmp, 2 * l)).reshape(2, LR, CB)
+                a[place] = spectrum
+            else:
+                spectrum = a[place]
+            tmp[place] = dot3(b2h[...], b2l[...], multiply(spectrum, b[place], conjugate)).reshape(2, LR, CB)
+
+        loop(1, LC // 2, step, ROWS)
 
     def columns_inv(k):
         return dot3(b1h[...], b1l[...], tmp[:, at(k, G), :].reshape(G * LC, CB))
@@ -260,7 +277,7 @@
 
     for copy in own_tables:
         copy.wait()
-    loop(0, CHUNKS, filt_step)
+    loop(0, CHUNKS, filt_step, COLS)
     ring(1)
     rows_fwd(fsp)
 
@@ -280,16 +297,15 @@
 
         return step
 
-    loop(0, CHUNKS, plane_step(mch))
-    rows_fwd(msp)
+    loop(0, CHUNKS, plane_step(mch), COLS)
     ring(3)
-    rows_inv(msp, fsp, False)
+    rows_product(msp, fsp, False, True)
 
     def conv_step(k):
         cmn[0, at(k, CH), :] = columns_inv(xl * (CHUNKS // 2) + k).astype(BF)
         cvo[at(k, CH), :] = columns_inv((1 - xl) * (CHUNKS // 2) + k).astype(BF)
 
-    loop(0, CHUNKS // 2, conv_step)
+    loop(0, CHUNKS // 2, conv_step, COLS // 2)
     conv_copy = remote(cvo, cmn.at[1], x_s.at[NZ], x_r.at[NZ], f, pr)
     conv_copy.start()
     for copy in own_gate:
@@ -406,29 +422,28 @@
 
     loop(0, FC, gwx_step)
 
-    def gw_copy(n, peer, sender):
-        return remote(gws.at[peer, n], gwr.at[n, sender], gw_s.at[n, peer], gw_r.at[n, sender], 2 * peer + core, (r, pr)[n])
-
-    def gw_step(j):
-        total = gw_partial(2 * j + core)
-        gwx_copy(j).wait_recv()
-        piece = (total + gwy[j].astype(F32)).astype(BF)
-        gws[j, 0] = piece[:CB]
-        gws[j, 1] = piece[CB:]
-        gw_copy(1, j, chip).start()
+    def gwy_copy(h, peer, sender):
+        return remote(gws.at[peer, h], gwr.at[sender, h], gw_s.at[h, peer], gw_r.at[h, sender], (xh * NY + peer) * 2 + core, r)
+
+    def gw_step(peer):
+        for h in range(NX):
+            j = h * NY + peer
+            total = gw_partial(2 * j + core)
+            gwx_copy(j).wait_recv()
+            gws[peer, h] = (total + gwy[j].astype(F32)).astype(BF)
 
     def gw_send_step(k):
-        j = lax.rem(chip + k, FC)
-        gw_step(j)
-        gw_copy(0, j, chip).start()
-
-    loop(1, FC, gw_send_step)
-    gw_step(chip)
+        peer = lax.rem(y + k, NY)
+        gw_step(peer)
+        for h in range(NX):
+            gwy_copy(h, peer, y).start()
+
+    loop(1, NY, gw_send_step)
+    gw_step(y)
 
     loop(0, NZ, lambda k: dconv_copy(k, 1 - xl).wait_recv())
-    loop(0, CHUNKS, plane_step(dch))
-    rows_fwd(dsp)
-    rows_inv(dsp, fsp, True)
+    loop(0, CHUNKS, plane_step(dch), COLS)
+    rows_product(dsp, fsp, True, True)
 
     def dm_copy(peer, sender):
         return remote(dms.at[at(peer, TB), :], dmt.at[:, at(sender, CB)], dm_s.at[peer], dm_r.at[sender], f, peer)
@@ -444,16 +459,35 @@
         for n in range(CH // TB):
             dm_send(chunk * (CH // TB) + n)
 
-    loop(0, CHUNKS, dmixed_step)
+    loop(0, CHUNKS, dmixed_step, COLS)
     own_dm = pltpu.make_async_copy(dms.at[at(r, TB), :], dmt.at[:, at(r, CB)], local.at[7])
     own_dm.start()
 
-    rows_inv(dsp, msp, True)
+    def gwz_copy(h, n):
+        return remote(gwp.at[h, n], gwq.at[h, n], gwz_s.at[h, n], gwz_r.at[h, n], (lax.rem(xh + h, NX) * NY + y) * 2 + core, (r, pr)[n])
+
+    def gw_over_y():
+        for h in range(NX):
+            block = lax.rem(xh + h, NX)
+            total = gws[y, block].astype(F32)
+            for k in range(1, NY):
+                sender = lax.rem(y + k, NY)
+                gwy_copy(block, y, sender).wait_recv()
+                total = total + gwr[sender, block].astype(F32)
+            if h == 0:
+                gw_out[...] = total[:CB]
+            else:
+                gwp[h, 0] = total[:CB].astype(BF)
+                gwz_copy(h, 0).start()
+            gwp[h, 1] = total[CB:].astype(BF)
+            gwz_copy(h, 1).start()
+
+    rows_product(dsp, msp, True, False)
 
     def gf_step(k):
         gff[at(k, CH), :] = columns_inv(k)
 
-    loop(0, CHUNKS, gf_step)
+    loop(0, CHUNKS, gf_step, COLS)
 
     def gfx_copy(j):
         return remote(gfx.at[j], gfy.at[j], gfx_s.at[j], gfx_r.at[j], twin, r)
@@ -478,21 +512,7 @@
 
     loop(1, FC, gf_send_step)
     gf_sum(chip)
-
-    gw_out[...] = gws[chip, 0].astype(F32)
-
-    def gw_add(n, sender):
-        gw_copy(n, chip, sender).wait_recv()
-        gw_out[...] += gwr[n, sender].astype(F32)
-
-    def gw_arrive(k):
-        sender = lax.rem(chip + FC - k, FC)
-        gw_add(0, sender)
-        gw_add(1, sender)
-
-    loop(1, FC, gw_arrive)
-    gw_add(1, chip)
-    gw_out[...] = gw_out[...] * (1.0 / F)
+    gw_over_y()
 
     gfr[chip] = gfs[chip]
     loop(1, FC, lambda k: gf_copy(chip, lax.rem(chip + FC - k, FC)).wait_recv())
@@ -501,6 +521,14 @@
         total = total + gfr[n].astype(F32)
     gf_out[...] = total.T * (1.0 / F)
 
+    total = gw_out[...]
+    for h in range(NX):
+        for n in range(2):
+            if h + n > 0:
+                gwz_copy(h, n).wait_recv()
+                total = total + gwq[h, n].astype(F32)
+    gw_out[...] = total * (1.0 / F)
+
     for copy in own_dg:
         copy.wait()
 
@@ -544,17 +572,25 @@
 
     def chip_sent(k):
         peer = lax.rem(chip + k, FC)
-        gw_copy(0, peer, chip).wait_send()
         gf_copy(peer, chip).wait_send()
 
     loop(1, FC, chip_sent)
 
     def twin_sent(j):
-        gw_copy(1, j, chip).wait_send()
         gwx_copy(j).wait_send()
         gfx_copy(j).wait_send()
 
     loop(0, FC, twin_sent)
+
+    def y_sent(k):
+        for h in range(NX):
+            gwy_copy(h, lax.rem(y + k, NY), y).wait_send()
+
+    loop(1, NY, y_sent)
+    for h in range(NX):
+        for n in range(2):
+            if h + n > 0:
+                gwz_copy(h, n).wait_send()
     w_copy(1, f, f).wait_send()
     conv_copy.wait_send()
 
@@ -578,6 +614,8 @@
     NZ = R // 2
     TB, CB, DB, PB = POS // R, D // R, D // F, POS // F
     CR = D * RIGHT // 16 // (128 * SUB) * (128 * SUB)
+    NX = 2 if F >= 8 else 1
+    NY = F // 2 // NX
     tables = [jnp.asarray(t) for t in build_tables()]
     vmem = pl.BlockSpec(memory_space=pltpu.VMEM)
     hbm = pl.BlockSpec(memory_space=pl.ANY)
@@ -615,7 +653,8 @@
             pltpu.VMEM((2, HALF, CB), BF),
             pltpu.VMEM((POS, CB), BF),
             pltpu.VMEM((F // 2, 2 * CB, DB), BF), pltpu.VMEM((F // 2, 2 * CB, DB), BF),
-            pltpu.VMEM((F // 2, 2, CB, DB), BF), pltpu.VMEM((2, F // 2, CB, DB), BF),
+            pltpu.VMEM((NY, NX, 2 * CB, DB), BF), pltpu.VMEM((NY, NX, 2 * CB, DB), BF),
+            pltpu.VMEM((NX, 2, CB, DB), BF), pltpu.VMEM((NX, 2, CB, DB), BF),
             pltpu.VMEM((POS, CB), F32),
             pltpu.VMEM((F // 2, PB, CB), BF), pltpu.VMEM((F // 2, PB, CB), BF),
             pltpu.VMEM((F // 2, PB, CB), BF), pltpu.VMEM((F // 2, PB, CB), BF),
@@ -627,7 +666,8 @@
             dma((NZ + 1,)), dma((NZ + 1,)),
             dma((2, NZ)), dma((R,)),
             dma((R,)), dma((R,)),
-            dma((F // 2,)), dma((F // 2,)), dma((2, F // 2)), dma((2, F // 2)),
+            dma((F // 2,)), dma((F // 2,)), dma((NX, NY)), dma((NX, NY)),
+            dma((NX, 2)), dma((NX, 2)),
             dma((F // 2,)), dma((F // 2,)), dma((F // 2,)), dma((F // 2,)),
         ],
         compiler_params=pltpu.CompilerParams(

time: 197 us -> 195 us (0.990)
  no operation moved by 1% of the time
where the time goes in v4:
time: 195 us; the launch traced here: 194 us
  Pallas kernels  193 us (99%)
    pallas_call x1, Pallas kernels, local(): pl.pallas_call(functools.partial(kernel, R, F, D, CR), out_shape=(jax.Sha...  189 us

profile of v4, /device:TPU:32, one launch (start us, length us, event | category | flops | bytes accessed | tf_op | source)
XLA Modules:
  0.0 193.7 jit_solution(8815850130797766565)
XLA Ops:
  0.6 189.1 %shard_map.175 = (bf16[128,4096]{1,0:T(8,128)(2,1)}, bf16[128,4096]{1,0:T(8,128)(2,1)}, f32[256,256]{1,0:T(8,128)}, f32[256,128]{1,0:T(8,128)}) custom-call(bf16[128,12288]{1,0:T(8,128)(2,1)} %bitcast.3, bf16[128,4096]{1,0:T(8,128)(2,1)} %bitcast.6, bf16[256,256]{1,0:T(8,128)(2,1)} %w.1, f32[256,2048]{1,0:T(8,128)} %filt_hbm.1, ...), custom_call_target="tpu_custom_call" | custom-call | tf_op jit(solution)/shard_map/pallas_call | solution.py:624
  189.7 3.9 %shard_map.176 = (bf16[128,12288]{1,0:T(8,128)(2,1)}, f32[256,256]{1,0:T(8,128)}, f32[256,128]{1,0:T(8,128)}) custom-call(bf16[128,12288]{1,0:T(8,128)(2,1)} %bitcast.4, bf16[128,12288]{1,0:T(8,128)(2,1)} %bitcast.5, bf16[128,4096]{1,0:T(8,128)(2,1)} %get-tuple-element.10.dmixed, bf16[128,4096]{1,0:T(8,128)(2,1)} %get-tuple-element.11.dgate, ...), custom_call_target="tpu_custom_call" | custom-call | tf_op jit(solution)/shard_map/pallas_call | solution.py:680

commit v5 on v4

--- a/solution.py
+++ b/solution.py
@@ -398,9 +398,11 @@
 
     for t in range(4, NZ):
         if t == NZ - 1:
+            ring(t)
             loop(2, NZ - 1, send_dg)
         step_done(t)
-        ring(t + 2)
+        if t + 2 < NZ - 1:
+            ring(t + 2)
     if NZ <= 4:
         loop(2, NZ - 1, send_dg)
     send_dg(1)
@@ -595,17 +597,42 @@
     conv_copy.wait_send()
 
 
-def finish(value, gate_a, dmixed, dgate, gw, gf, out, gw_out, gf_out):
-    D = dmixed.shape[1]
-    d = dmixed[...].astype(F32)
-    out[:, :D] = (d * gate_a[...].astype(F32)).astype(BF)
-    out[:, D : 2 * D] = (d * value[...].astype(F32)).astype(BF)
-    out[:, 2 * D :] = dgate[...]
-
-    @pl.when(pl.program_id(0) == 0)
-    def _():
-        gw_out[...] = gw[...]
-        gf_out[...] = gf[...]
+def finish(parts, proj, dmixed, dgate, gw, gf, out, gw_out, gf_out, factors, d, grads, gw_held, gf_held, load, store):
+    TB, D = dmixed.shape
+    rows = TB // parts
+    loads = []
+    for n in range(parts):
+        place = pl.ds(n * rows, rows)
+        loads.append((
+            pltpu.make_async_copy(proj.at[place, pl.ds(0, 2 * D)], factors.at[place, :], load.at[0, n]),
+            pltpu.make_async_copy(dmixed.at[place, :], d.at[place, :], load.at[1, n]),
+            pltpu.make_async_copy(dgate.at[place, :], grads.at[place, pl.ds(2 * D, D)], load.at[2, n]),
+        ))
+    loads.append((
+        pltpu.make_async_copy(gw, gw_held, load.at[0, parts]),
+        pltpu.make_async_copy(gf, gf_held, load.at[1, parts]),
+    ))
+    for group in loads:
+        for copy in group:
+            copy.start()
+    stores = []
+    for n in range(parts):
+        place = pl.ds(n * rows, rows)
+        for copy in loads[n]:
+            copy.wait()
+        x = d[place, :].astype(F32)
+        grads[place, :D] = (x * factors[place, D:].astype(F32)).astype(BF)
+        grads[place, D : 2 * D] = (x * factors[place, :D].astype(F32)).astype(BF)
+        stores.append(pltpu.make_async_copy(grads.at[place, :], out.at[place, :], store.at[n]))
+        stores[-1].start()
+    for copy in loads[parts]:
+        copy.wait()
+    stores.append(pltpu.make_async_copy(gw_held, gw_out, store.at[parts]))
+    stores.append(pltpu.make_async_copy(gf_held, gf_out, store.at[parts + 1]))
+    for copy in stores[parts:]:
+        copy.start()
+    for copy in stores:
+        copy.wait()
 
 
 def local(R, F, proj, dout, filt, w):
@@ -675,26 +702,26 @@
         ),
     )(proj, dout, w, filt, *tables)
     dmixed, dgate, gw, gf = grads
-    rows = TB // 2
-    whole = lambda *shape: pl.BlockSpec(shape, lambda i: (0, 0))
+    parts = 4
     grad_proj, gw, gf = pl.pallas_call(
-        finish,
-        grid=(TB // rows,),
+        functools.partial(finish, parts),
         out_shape=(
             jax.ShapeDtypeStruct((TB, 3 * D), BF),
             jax.ShapeDtypeStruct((CB, DB), F32),
             jax.ShapeDtypeStruct((CB, PB), F32),
         ),
-        in_specs=[
-            pl.BlockSpec((rows, D), lambda i: (i, 0)),
-            pl.BlockSpec((rows, D), lambda i: (i, 1)),
-            pl.BlockSpec((rows, D), lambda i: (i, 0)),
-            pl.BlockSpec((rows, D), lambda i: (i, 0)),
-            whole(CB, DB),
-            whole(CB, PB),
+        in_specs=[hbm] * 5,
+        out_specs=(hbm, hbm, hbm),
+        scratch_shapes=[
+            pltpu.VMEM((TB, 2 * D), BF),
+            pltpu.VMEM((TB, D), BF),
+            pltpu.VMEM((TB, 3 * D), BF),
+            pltpu.VMEM((CB, DB), F32),
+            pltpu.VMEM((CB, PB), F32),
+            dma((3, parts + 1)), dma((parts + 2,)),
         ],
-        out_specs=(pl.BlockSpec((rows, 3 * D), lambda i: (i, 0)), whole(CB, DB), whole(CB, PB)),
-    )(proj, proj, dmixed, dgate, gw, gf)
+        compiler_params=pltpu.CompilerParams(vmem_limit_bytes=62 * 1024 * 1024),
+    )(proj, dmixed, dgate, gw, gf)
     return grad_proj[None], gw, gf
 
 

time: 195 us -> 193 us (0.990)
  Pallas kernels: 193 us -> 191 us
where the time goes in v5:
time: 193 us; the launch traced here: 192 us
  Pallas kernels  191 us (99%)
    pallas_call x1, Pallas kernels, local(): pl.pallas_call(functools.partial(kernel, R, F, D, CR), out_shape=(jax.Sha...  187 us

profile of v5, /device:TPU:32, one launch (start us, length us, event | category | flops | bytes accessed | tf_op | source)
XLA Modules:
  0.0 191.6 jit_solution(5698954369103256871)
XLA Ops:
  0.6 187.4 %shard_map.175 = (bf16[128,4096]{1,0:T(8,128)(2,1)}, bf16[128,4096]{1,0:T(8,128)(2,1)}, f32[256,256]{1,0:T(8,128)}, f32[256,128]{1,0:T(8,128)}) custom-call(bf16[128,12288]{1,0:T(8,128)(2,1)} %bitcast.3, bf16[128,4096]{1,0:T(8,128)(2,1)} %bitcast.5, bf16[256,256]{1,0:T(8,128)(2,1)} %w.1, f32[256,2048]{1,0:T(8,128)} %filt_hbm.1, ...), custom_call_target="tpu_custom_call" | custom-call | tf_op jit(solution)/shard_map/pallas_call | solution.py:651
  188.0 3.4 %shard_map.176 = (bf16[128,12288]{1,0:T(8,128)(2,1)}, f32[256,256]{1,0:T(8,128)}, f32[256,128]{1,0:T(8,128)}) custom-call(bf16[128,12288]{1,0:T(8,128)(2,1)} %bitcast.4, bf16[128,4096]{1,0:T(8,128)(2,1)} %get-tuple-element.10.dmixed, bf16[128,4096]{1,0:T(8,128)(2,1)} %get-tuple-element.11.dgate, f32[256,256]{1,0:T(8,128)} %get-tuple-element.12.gw, ...), custom_call_target="tpu_custom_call" | custom-call | tf_op jit(solution)/shard_map/pallas_call | solution.py:706

commit v6 on v5

--- a/solution.py
+++ b/solution.py
@@ -79,8 +79,8 @@
 def kernel(
     R, F, D, CR,
     proj, dout, w, filt_hbm, t0, t1, t2, t3, t4, t5, t6, t7, t8, t9, t10, t11,
-    dmt, dgt, gw_out, gf_out,
-    filt, a1h, a1l, a2h, a2l, azh, azl, b2h, b2l, bzh, bzl, b1h, b1l,
+    dmt, dgt, gw_hbm, gf_hbm,
+    gw_out, gf_out, filt, a1h, a1l, a2h, a2l, azh, azl, b2h, b2l, bzh, bzl, b1h, b1l,
     value, gate_a, mx, mch, gmn, cmn, cvo, dh, w2, fsp, msp, dsp, tmp, acc, gt, dcv, dch, dg, dms,
     gwx, gwy, gws, gwr, gwp, gwq, gff, gfx, gfy, gfs, gfr,
     local, ring_s, ring_r, mx_s, mx_r, gate_s, gate_r, w_s, w_r, x_s, x_r, dg_s, dg_r, dm_s, dm_r,
@@ -530,6 +530,12 @@
                 gwz_copy(h, n).wait_recv()
                 total = total + gwq[h, n].astype(F32)
     gw_out[...] = total * (1.0 / F)
+    sums_out = [
+        pltpu.make_async_copy(gw_out, gw_hbm, local.at[23]),
+        pltpu.make_async_copy(gf_out, gf_hbm, local.at[24]),
+    ]
+    for copy in sums_out:
+        copy.start()
 
     for copy in own_dg:
         copy.wait()
@@ -541,6 +547,8 @@
 
     loop(1, NZ, dg_arrive)
 
+    for copy in sums_out:
+        copy.wait()
     own_dm.wait()
     loop(1, R, lambda k: dm_copy(r, lax.rem(r + R - k, R)).wait_recv())
 
@@ -644,7 +652,6 @@
     NX = 2 if F >= 8 else 1
     NY = F // 2 // NX
     tables = [jnp.asarray(t) for t in build_tables()]
-    vmem = pl.BlockSpec(memory_space=pltpu.VMEM)
     hbm = pl.BlockSpec(memory_space=pl.ANY)
     dma = pltpu.SemaphoreType.DMA
     spectrum = pltpu.VMEM((LC + 2, LR, CB), F32)
@@ -659,8 +666,9 @@
         in_specs=[
             hbm, hbm, hbm, hbm,
         ] + [hbm] * len(tables),
-        out_specs=(hbm, hbm, vmem, vmem),
+        out_specs=(hbm, hbm, hbm, hbm),
         scratch_shapes=[
+            pltpu.VMEM((CB, DB), F32), pltpu.VMEM((CB, PB), F32),
             pltpu.VMEM((CB, POS), F32),
         ] + [pltpu.VMEM(t.shape, BF) for t in tables] + [
             pltpu.VMEM((TB, D), BF), pltpu.VMEM((TB, D), BF),
@@ -685,7 +693,7 @@
             pltpu.VMEM((POS, CB), F32),
             pltpu.VMEM((F // 2, PB, CB), BF), pltpu.VMEM((F // 2, PB, CB), BF),
             pltpu.VMEM((F // 2, PB, CB), BF), pltpu.VMEM((F // 2, PB, CB), BF),
-            dma((23,)),
+            dma((25,)),
             dma((2 * SUB, NZ)), dma((2 * SUB, NZ)),
             dma((R,)), dma((R,)),
             dma((2, NZ)), dma((2, NZ)),
@@ -702,7 +710,7 @@
         ),
     )(proj, dout, w, filt, *tables)
     dmixed, dgate, gw, gf = grads
-    parts = 4
+    parts = 2
     grad_proj, gw, gf = pl.pallas_call(
         functools.partial(finish, parts),
         out_shape=(

time: 193 us -> 193 us (level)
  no operation moved by 1% of the time
where the time goes in v6:
time: 193 us; the launch traced here: 191 us
  Pallas kernels  190 us (98%)
    pallas_call x1, Pallas kernels, local(): pl.pallas_call(functools.partial(kernel, R, F, D, CR), out_shape=(jax.Sha...  187 us

profile of v6, /device:TPU:32, one launch (start us, length us, event | category | flops | bytes accessed | tf_op | source)
XLA Modules:
  0.0 191.2 jit_solution(11049389990835137248)
XLA Ops:
  0.6 186.6 %shard_map.175 = (bf16[128,4096]{1,0:T(8,128)(2,1)}, bf16[128,4096]{1,0:T(8,128)(2,1)}, f32[256,256]{1,0:T(8,128)}, f32[256,128]{1,0:T(8,128)}) custom-call(bf16[128,12288]{1,0:T(8,128)(2,1)} %bitcast.3, bf16[128,4096]{1,0:T(8,128)(2,1)} %bitcast.5, bf16[256,256]{1,0:T(8,128)(2,1)} %w.1, f32[256,2048]{1,0:T(8,128)} %filt_hbm.1, ...), custom_call_target="tpu_custom_call" | custom-call | tf_op jit(solution)/shard_map/pallas_call | solution.py:658
  187.3 3.7 %shard_map.176 = (bf16[128,12288]{1,0:T(8,128)(2,1)}, f32[256,256]{1,0:T(8,128)}, f32[256,128]{1,0:T(8,128)}) custom-call(bf16[128,12288]{1,0:T(8,128)(2,1)} %bitcast.4, bf16[128,4096]{1,0:T(8,128)(2,1)} %get-tuple-element.10.dmixed, bf16[128,4096]{1,0:T(8,128)(2,1)} %get-tuple-element.11.dgate, f32[256,256]{1,0:T(8,128)} %get-tuple-element.12.gw, ...), custom_call_target="tpu_custom_call" | custom-call | tf_op jit(solution)/shard_map/pallas_call | solution.py:714
